TPU v7x, 256 devices: a whole 4x4x8 slice. The times are simulated.
256 devices in a mesh: tgt: 8 (over z_hi, core), row: 8 (over z_lo, x), col: 4 (over y).
Axes of the slice: x: 4, y: 4, z: 8 (z_hi: 4, z_lo: 2; z = z_hi * 2 + z_lo), core: 2. Of those that a mesh axis runs over, the one named last changes fastest.
Arguments:
- homolog_activation_matrix: bfloat16 [8, 128, 512, 256], P('tgt', None, ('row', 'col')), may hold values from -80 to 80
- standardizer_multiplier: float32 [256], replicated, may hold values from 0.5 to 1.5
- standardizer_offset: float32 [256], replicated, may hold values from -3 to 3
- side_mapping_matrices: bfloat16 [256, 64], replicated, may hold values from -0.375 to 0.375
- side_mapping_offsets: float32 [64], replicated, may hold values from -3 to 3
- final_channel_matrix: bfloat16 [1024, 128], replicated, may hold values from -0.1875 to 0.1875
- residue_couple_cotangent: bfloat16 [8, 512, 512, 128], P('tgt', 'row', 'col'), may hold values from -32.4 to 32.4
Outputs:
- sequence_stack_cotangent: bfloat16 [8, 128, 512, 256], P('tgt', None, ('row', 'col'))
- proj_weight_grad: float32 [256, 64], replicated
- proj_bias_grad: float32 [64], replicated
- ln_gain_grad: float32 [256], replicated
- ln_bias_grad: float32 [256], replicated
- out_weight_grad: float32 [1024, 128], replicated
- out_bias_grad: float32 [128], replicated
All inputs are finite; a program needn't handle non-finite values.
Results may differ from a plain program's by a relative error of at most 0.0069.
Values may be sent and summed in bfloat16 or wider, within the bound.
A program may use at most 128 MiB of HBM per device.

v0:
```python
import math

import jax
import jax.numpy as jnp
from jax import lax
from jax.sharding import PartitionSpec as P

CM = 256
CH = 32
CZ = 128
S = 128


def per_device(
    homolog_activation_matrix,
    standardizer_multiplier,
    standardizer_offset,
    side_mapping_matrices,
    side_mapping_offsets,
    final_channel_matrix,
    residue_couple_cotangent,
):
    row_count = lax.axis_size("row")
    col_count = lax.axis_size("col")
    col_index = lax.axis_index("col")
    channel_entries = homolog_activation_matrix[0].astype(jnp.float32)
    res_local = channel_entries.shape[1]
    full_res = res_local * row_count * col_count
    centre = jnp.mean(channel_entries, -1, keepdims=True)
    centred = channel_entries - centre
    inverse_deviation = lax.rsqrt(jnp.mean(centred * centred, -1, keepdims=True) + 1e-05)
    normalized_input = centred * inverse_deviation
    norm_result = (normalized_input * standardizer_multiplier + standardizer_offset).astype(
        jnp.bfloat16
    )
    flat_out = norm_result.reshape(S * res_local, CM)
    projected = (
        jnp.dot(flat_out, side_mapping_matrices, preferred_element_type=jnp.float32)
        + side_mapping_offsets
    ).astype(jnp.bfloat16)
    projected = projected.reshape(S, res_local, 2 * CH)
    grads = residue_couple_cotangent[0]
    rows_here = grads.shape[0]
    cols_here = grads.shape[1]
    left_panel = lax.all_gather(projected[..., :CH], "col", axis=1, tiled=True)
    right_whole = lax.all_gather(projected[..., CH:], ("row", "col"), axis=1, tiled=True)
    right_panel = lax.dynamic_slice_in_dim(right_whole, col_index * cols_here, cols_here, 1)
    block_rows = math.gcd(rows_here, 16)

    def block_step(running, row_start):
        right_acc, wide_accumulator = running
        grad_block = lax.dynamic_slice_in_dim(grads, row_start, block_rows, 0)
        left_block = lax.dynamic_slice_in_dim(left_panel, row_start, block_rows, 1)
        pair_back = jnp.einsum(
            "ije,ke->ijk", grad_block, final_channel_matrix, preferred_element_type=jnp.float32
        )
        pair_back = pair_back.astype(jnp.bfloat16).reshape(block_rows, cols_here, CH, CH)
        row_grad = (
            jnp.einsum("ijcd,sjd->sic", pair_back, right_panel, preferred_element_type=jnp.float32)
            / S
        )
        right_acc = right_acc + jnp.einsum(
            "ijcd,sic->sjd", pair_back, left_block, preferred_element_type=jnp.float32
        )
        outer = (
            jnp.einsum("sic,sjd->ijcd", left_block, right_panel, preferred_element_type=jnp.float32)
            / S
        )
        outer = outer.astype(jnp.bfloat16).reshape(block_rows, cols_here, CH * CH)
        wide_accumulator = wide_accumulator + jnp.einsum(
            "ijk,ije->ke", outer, grad_block, preferred_element_type=jnp.float32
        )
        return ((right_acc, wide_accumulator), row_grad)

    starts = jnp.arange(rows_here // block_rows, dtype=jnp.int32) * block_rows
    initial = (jnp.zeros((S, cols_here, CH), jnp.float32), jnp.zeros((CH * CH, CZ), jnp.float32))
    (right_acc, wide_accumulator), row_blocks = lax.scan(block_step, initial, starts)
    left_partial = jnp.moveaxis(row_blocks, 0, 1).reshape(S, rows_here, CH)
    right_partial = right_acc / S
    embedded = jnp.zeros((S, full_res, CH), jnp.float32)
    embedded = lax.dynamic_update_slice_in_dim(embedded, right_partial, col_index * cols_here, 1)
    left_own = lax.psum_scatter(left_partial, "col", scatter_dimension=1, tiled=True)
    right_own = lax.psum_scatter(embedded, ("row", "col"), scatter_dimension=1, tiled=True)
    side_grad = jnp.concatenate([left_own, right_own], -1)
    side_round = side_grad.astype(jnp.bfloat16)
    flat_side = side_round.reshape(S * res_local, 2 * CH)
    norm_out_grad = jnp.einsum(
        "nk,ck->nc", flat_side, side_mapping_matrices, preferred_element_type=jnp.float32
    ).reshape(S, res_local, CM)
    weight_component = jnp.einsum(
        "nc,nk->ck", flat_out, flat_side, preferred_element_type=jnp.float32
    )
    bias_component = jnp.sum(side_grad, (0, 1))
    gain_component = jnp.sum(norm_out_grad * normalized_input, (0, 1))
    shift_component = jnp.sum(norm_out_grad, (0, 1))
    scaled_values = norm_out_grad * standardizer_multiplier
    alignment_backward = inverse_deviation * (
        scaled_values
        - jnp.mean(scaled_values, -1, keepdims=True)
        - normalized_input * jnp.mean(scaled_values * normalized_input, -1, keepdims=True)
    )
    sequence_stack_cotangent = alignment_backward.astype(jnp.bfloat16)[None]
    output_bias_component = jnp.sum(grads.astype(jnp.float32), (0, 1))
    factor_all = 1.0 / (lax.axis_size("tgt") * full_res)
    addend_contributions = (
        weight_component * factor_all,
        bias_component * factor_all,
        gain_component * factor_all,
        shift_component * factor_all,
        wide_accumulator * factor_all,
        output_bias_component * factor_all,
    )
    running_totals = lax.psum(
        (
            addend_contributions[0],
            addend_contributions[1],
            addend_contributions[2],
            addend_contributions[3],
            addend_contributions[4],
            addend_contributions[5],
        ),
        ("tgt", "row", "col"),
    )
    return (
        sequence_stack_cotangent,
        running_totals[0],
        running_totals[1],
        running_totals[2],
        running_totals[3],
        running_totals[4],
        running_totals[5],
    )


def solution(mesh):
    placed = (
        P("tgt", None, ("row", "col"), None),
        P(),
        P(),
        P(),
        P(),
        P(),
        P("tgt", "row", "col", None),
    )
    return jax.shard_map(
        per_device,
        mesh=mesh,
        in_specs=placed,
        out_specs=(P("tgt", None, ("row", "col"), None), P(), P(), P(), P(), P(), P()),
        check_vma=False,
    )
```

profile of v0, /device:TPU:1, one launch (start us, length us, event | category | flops | bytes accessed | tf_op | source)
XLA Modules:
  0.0 864.8 jit_solution(14439627092193007857)
XLA Ops:
  7.2 1.7 convert_reduce_fusion.1
  8.9 1.9 multiply_reduce_fusion.2
  15.6 26.3 %all_gather.6 = bf16[128,64,32]{2,1,0:T(8,128)(2,1)} all-gather(bf16[128,16,32]{2,1,0:T(8,128)(2,1)S(1)} %get-tuple-element.166), channel_id=1, replica_groups=mesh['tgt'=8,'row'=8,'col'=4] {'col'}, dimensions={1}, use_global_device_ids=true | all-gather | bytes 655360 | tf_op jit(solution)/shard_map/all_gather | solution.py:45
  41.9 3.9 copy.44
  45.8 205.2 %all-gather.2.cloned.1.call-done = bf16[128,512,32]{2,1,0:T(8,128)(2,1)} async-done(((bf16[128,16,32]{2,1,0:T(8,128)(2,1)}), bf16[128,512,32]{2,1,0:T(8,128)(2,1)}) %all-gather.2.cloned.1.call-update) | async-done | bytes 4194320 | tf_op jit(solution)/shard_map/all_gather | solution.py:46
  251.0 4.7 constant_dynamic-slice_fusion
  255.7 4.0 copy.45
  259.8 106.7 %while.15 = (s32[]{:T(128)}, f32[128,128,32]{1,0,2:T(8,128)S(1)}, f32[1024,128]{1,0:T(8,128)}, f32[4,128,16,32]{1,3,2,0:T(8,128)}, s32[4]{0:T(128)S(1)}, /*index...) while((s32[]{:T(128)}, f32[128,128,32]{1,0,2:T(8,128)S(1)}, ...), condition=%wide.region_3.4_spmd.clone, body=%wide.region_2.3_spmd.clone.sunk | while | flops 2692022272 | bytes 67896080 | solution.py:77
  262.3 4.2 convolution_convert_fusion.2
  266.5 6.4 copy.81
  272.9 4.2 bitcast_add_fusion.2
  277.1 2.2 fusion.76
  279.3 1.8 copy.82
  281.1 2.6 fusion.77
  284.5 2.0 fusion.78
  289.0 4.2 convolution_convert_fusion.2
  293.2 6.4 copy.81
  299.6 4.2 bitcast_add_fusion.2
  303.8 2.2 fusion.76
  306.0 1.8 copy.82
  307.7 2.6 fusion.77
  311.1 2.0 fusion.78
  315.7 4.2 convolution_convert_fusion.2
  319.9 6.4 copy.81
  326.3 4.2 bitcast_add_fusion.2
  330.5 2.2 fusion.76
  332.6 1.8 copy.82
  334.4 2.6 fusion.77
  337.8 2.0 fusion.78
  342.4 4.2 convolution_convert_fusion.2
  346.6 6.4 copy.81
  353.0 4.2 bitcast_add_fusion.2
  357.1 2.2 fusion.76
  359.3 1.8 copy.82
  361.1 2.6 fusion.77
  364.5 2.0 fusion.78
  366.8 2.0 copy.46
  368.8 4.3 broadcast_in_dim.30
  373.1 1.6 multiply_dynamic-update-slice_fusion
  378.3 34.9 %reduce-scatter.3.cloned.1.call-done = f32[128,16,32]{0,2,1:T(8,128)} async-done(((f32[128,64,32]{0,2,1:T(8,128)}), f32[128,16,32]{0,2,1:T(8,128)}) %reduce-scatter.3.cloned.1.call-update) | async-done | bytes 262160 | tf_op jit(solution)/shard_map/reduce_scatter | solution.py:82
  413.2 1.7 constant_dynamic-update-slice_fusion.1
  414.9 162.3 %reduce-scatter.5.cloned.1.call-done = f32[128,16,32]{0,2,1:T(8,128)} async-done(((f32[128,512,32]{0,2,1:T(8,128)}), f32[128,16,32]{0,2,1:T(8,128)}) %reduce-scatter.5.cloned.1.call-update) | async-done | bytes 262160 | tf_op jit(solution)/shard_map/reduce_scatter | solution.py:83
  577.1 1.7 constant_dynamic-update-slice_fusion
  578.8 3.1 multiply_reduce_fusion
  583.1 2.5 fusion.39
  588.6 96.5 %all-reduce = (f32[64]{0:T(128)}, f32[256]{0:T(256)}, f32[256]{0:T(256)}, f32[128]{0:T(128)}) all-reduce(f32[64]{0:T(128)S(1)} %broadcast_multiply_fusion.7, f32[256]{0:T(256)S(1)} %get-tuple-element.171, f32[256]{0:T(256)S(1)} %get-tuple-element.170, ...), channel_id=1, replica_groups=mesh['tgt'=8,'row'=8,'col'=4] {'tgt','row','col'}, use_global_device_ids=true, to_apply=%region_10.11 | all-reduce | flops 704 | bytes 5632 | tf_op jit(solution)/shard_map/psum | solution.py:113
  685.0 169.9 %all-reduce.4.cloned.1.call-done = (f32[256,64]{0,1:T(8,128)}, f32[1024,128]{1,0:T(8,128)}) async-done(((f32[256,64]{0,1:T(8,128)}, f32[1024,128]{1,0:T(8,128)}), (f32[256,64]{0,1:T(8,128)}, f32[1024,128]{1,0:T(8,128)})) %all-reduce.4.cloned.1.call-update) | async-done | bytes 589840 | tf_op jit(solution)/shard_map/psum | solution.py:113
  856.4 1.9 copy.101
  (82 shorter events, 19.6 us)
Async XLA Ops:
  7.2 6.6 copy-start
  7.2 3.8 copy-start.6
  7.2 243.8 %all-gather.2.cloned.1.call-start = ((), (), s32[]{:S(2)}) async-start(), calls=%async_computation.2 | async-start | bytes 17301504 | tf_op jit(solution)/shard_map/all_gather | solution.py:46
  11.6 1.2 copy-start.10
  11.6 1.2 copy-start.11
  12.8 0.9 copy-start.12
  15.5 397.7 %reduce-scatter.3.cloned.1.call-start = ((), (), s32[]{:S(2)}) async-start(), calls=%async_computation.3 | async-start | bytes 1310720 | tf_op jit(solution)/shard_map/reduce_scatter | solution.py:82
  255.7 4.0 copy-start.9
  279.3 1.8 copy-start.3
  281.1 3.4 copy-start.1
  283.7 0.8 copy-start.4
  305.9 1.8 copy-start.3
  307.7 3.4 copy-start.1
  310.3 0.8 copy-start.4
  332.6 1.8 copy-start.3
  334.4 3.4 copy-start.1
  337.0 0.8 copy-start.4
  359.3 1.8 copy-start.3
  361.1 3.4 copy-start.1
  363.7 0.8 copy-start.4
  366.5 210.6 %reduce-scatter.5.cloned.1.call-start = ((), (), s32[]{:S(2)}) async-start(), calls=%async_computation.4 | async-start | bytes 8650752 | tf_op jit(solution)/shard_map/reduce_scatter | solution.py:83
  368.8 4.3 copy-start.8
  374.7 1.6 copy-start.2
  374.7 2.7 copy-start.5
  374.7 480.2 %all-reduce.4.cloned.1.call-start = ((), (), s32[]{:S(2)}) async-start(), calls=%async_computation.5 | async-start | bytes 1179648 | tf_op jit(solution)/shard_map/psum | solution.py:113
  377.4 201.4 %copy-start.7 = (bf16[1,128,16,256]{3,2,1,0:T(8,128)(2,1)S(1)}, bf16[1,128,16,256]{3,2,1,0:T(8,128)(2,1)}, u32[]{:S(2)}) copy-start(bf16[1,128,16,256]{3,2,1,0:T(8,128)(2,1)} %param.9) | copy-start | bytes 3145732
Sparse Core Ops, SparseCore 0:
  15.6 235.3 all-gather.1
  366.6 46.5 reduce-scatter.2
  415.9 161.1 reduce-scatter.4
  585.7 269.1 all-reduce.3
where the time goes:
time: 866 us; the launch traced here: 865 us
  waiting for transfers between devices  572 us (66%)
  blocking collectives  123 us (14%)
  local copies, waits for them, and re-layouts  69.8 us (8%)
  matrix products  66.6 us (8%)
  between operations  14 us (2%)
  other arithmetic  10.9 us (1%)
    all_gather x1, waiting for transfers between devices, per_device(): lax.all_gather(projected[..., CH:], ('row', 'col'), axis=1, tiled=True)  205 us
    psum x1, waiting for transfers between devices, per_device(): lax.psum((addend_contributions[0], addend_contributions[1], addend_contri...  170 us
    reduce_scatter x1, waiting for transfers between devices, per_device(): lax.psum_scatter(embedded, ('row', 'col'), scatter_dimension=1, tiled=True)  162 us
    psum x1, blocking collectives, per_device(): lax.psum((addend_contributions[0], addend_contributions[1], addend_contri...  96.5 us
    reduce_scatter x1, waiting for transfers between devices, per_device(): lax.psum_scatter(left_partial, 'col', scatter_dimension=1, tiled=True)  34.9 us
    all_gather x1, blocking collectives, per_device(): left_panel = lax.all_gather(projected[..., :CH], 'col', axis=1, tiled=True)  26.3 us
    convert_element_type x4, local copies, waits for them, and re-layouts, block_step(): pair_back.astype(jnp.bfloat16).reshape(block_rows, cols_here, CH, CH)  25.6 us
  transfers between devices with their start and end apart: 4, of which 4 were waited for; matrix products, arithmetic and copies ran while one was open for 2% of the time, Pallas kernels for 0%

commit v1 on v0

v1 whole, which is shorter than its diff:
```python
import functools

import jax
import jax.numpy as jnp
from jax import lax
from jax.experimental import pallas as pl
from jax.experimental.pallas import tpu as pltpu
from jax.sharding import PartitionSpec as P

CM = 256
CH = 32
CZ = 128
S = 128
F32 = jnp.float32
BF16 = jnp.bfloat16
NT_DIMS = (((1,), (1,)), ((), ()))
NN_DIMS = (((1,), (0,)), ((), ()))


def mm(a, b, dims=NN_DIMS):
    return lax.dot_general(a, b, dims, preferred_element_type=F32)


def axis_sizes():
    return lax.axis_size("tgt"), lax.axis_size("row"), lax.axis_size("col")


def axis_places():
    return lax.axis_index("tgt"), lax.axis_index("row"), lax.axis_index("col")


def descriptor(src, dst, send, recv, where):
    return pltpu.make_async_remote_copy(
        src_ref=src,
        dst_ref=dst,
        send_sem=send,
        recv_sem=recv,
        device_id=where,
        device_id_type=pl.DeviceIdType.MESH,
    )


def push(*args):
    descriptor(*args).start()


def sent(*args):
    descriptor(*args).wait_send()


def arrived(*args):
    descriptor(*args).wait_recv()


def greet(nt, nr, nc, t, r, c):
    barrier = pltpu.get_barrier_semaphore()
    flat = r * nc + c
    for k in range(1, nr * nc):
        other = lax.rem(flat + k, nr * nc)
        pl.semaphore_signal(
            barrier,
            inc=1,
            device_id={"row": other // nc, "col": lax.rem(other, nc)},
            device_id_type=pl.DeviceIdType.MESH,
        )
    for k in range(1, nt):
        pl.semaphore_signal(
            barrier,
            inc=1,
            device_id={"tgt": lax.rem(t + k, nt)},
            device_id_type=pl.DeviceIdType.MESH,
        )


def meet(nt, nr, nc):
    pl.semaphore_wait(pltpu.get_barrier_semaphore(), nr * nc - 1 + nt - 1)


def kernel(
    sizes,
    h_ref,
    mult_ref,
    off_ref,
    pm_ref,
    pb_ref,
    w_ref,
    g_ref,
    dx_out,
    pw_out,
    pbias_out,
    gain_out,
    shift_out,
    ow_out,
    ob_out,
    h,
    g,
    nrm,
    inv,
    no,
    lt,
    lmat,
    rt,
    rown,
    rf,
    wf,
    wp,
    pair,
    rp,
    lp,
    rr,
    lr,
    side,
    on,
    dw,
    obacc,
    a1,
    s1,
    a2,
    a3,
    a4,
    a5,
    pwt,
    vec,
    acc,
    sb,
    b1,
    b2,
    b3,
    b4,
    local_sem,
    gl_send,
    gl_recv,
    gr_send,
    gr_recv,
    sl_send,
    sl_recv,
    sr_send,
    sr_recv,
    a_row_send,
    a_row_recv,
    a_col_send,
    a_col_recv,
    a_tgt_send,
    a_tgt_recv,
    a_col2_send,
    a_col2_recv,
    a_row2_send,
    a_row2_recv,
    b_row_send,
    b_row_recv,
    b_col_send,
    b_col_recv,
    b_tgt_send,
    b_tgt_recv,
    b_row2_send,
    b_row2_recv,
):
    nt, nr, nc, rl = sizes
    rpc = nr // nc
    ni, nj = rl * nc, rl * nr
    lrows = rl * CH
    t, r, c = axis_places()
    home = lax.div(r, rpc)
    block = lax.rem(r, rpc) * nc + c
    mine = c == home

    h_in = pltpu.make_async_copy(h_ref, h, local_sem.at[0])
    h_in.start()
    g_in = pltpu.make_async_copy(g_ref, g, local_sem.at[1])
    g_in.start()
    greet(nt, nr, nc, t, r, c)

    mult = mult_ref[...]
    off = off_ref[...]
    pt32 = pm_ref[...].astype(F32).T
    pt = pt32.astype(BF16)
    bias = jnp.broadcast_to(pb_ref[...], (S, 2 * CH)).T

    wf[...] = w_ref[...].astype(F32)

    def reorder(d, _):
        rows = wf[pl.ds(d, CH, stride=CH), :]
        wp[pl.ds(pl.multiple_of(d * CH, CH), CH), :] = rows.astype(BF16)
        return 0

    lax.fori_loop(0, CH, reorder, 0)
    h_in.wait()

    def normalise(k, _):
        rows = pl.ds(pl.multiple_of(k * 128, 128), 128)
        x = h[rows, :].astype(F32)
        centred = x - jnp.mean(x, -1, keepdims=True)
        scale = lax.rsqrt(jnp.mean(centred * centred, -1, keepdims=True) + 1e-05)
        x = centred * scale
        nrm[0, rows, :] = x[:, :128]
        nrm[1, rows, :] = x[:, 128:]
        inv[rows, :] = jnp.broadcast_to(scale, (128, 128))
        return 0

    lax.fori_loop(0, S * rl // 128, normalise, 0)

    def project(k, _):
        at = pl.ds(k, S, stride=rl)
        x = jnp.concatenate([nrm[0, at, :], nrm[1, at, :]], 1)
        row = (x * mult + off).astype(BF16)
        no[pl.ds(pl.multiple_of(k * S, S), S), :] = row
        y = (mm(pt, row, NT_DIMS) + bias).astype(BF16)
        lt[pl.ds(pl.multiple_of(c * lrows + k * CH, CH), CH), :] = y[:CH]
        rf[pl.ds(pl.multiple_of(k * CH, CH), CH), :] = y[CH:].astype(F32)
        return 0

    lax.fori_loop(0, rl, project, 0)

    def turn(d, _):
        rown[d] = rf[pl.ds(d, rl, stride=CH), :].astype(BF16)
        return 0

    lax.fori_loop(0, CH, turn, 0)
    meet(nt, nr, nc)

    def left_block(k):
        return lt.at[pl.ds(pl.multiple_of(k * lrows, lrows), lrows), :]

    def right_block(k):
        return rt.at[:, pl.ds(pl.multiple_of(k * rl, rl), rl), :]

    def gather_left(k):
        q = lax.rem(c + k, nc)
        return left_block(c), left_block(c), gl_send.at[k], gl_recv.at[c], {"col": q}

    def gather_left_in(k):
        q = lax.rem(c + k, nc)
        return left_block(q), left_block(q), gl_send.at[k], gl_recv.at[q], {"col": q}

    def gather_right(k):
        q = lax.rem(r + k, nr)
        where = {"row": q, "col": home}
        return rown, right_block(block), gr_send.at[k], gr_recv.at[block], where

    def gather_right_in(k):
        where = {"row": rpc * c + k // nc, "col": k % nc}
        return rown, right_block(k), gr_send.at[0], gr_recv.at[k], where

    for k in range(1, nc):
        push(*gather_left(k))
    for k in range(1, nr):
        push(*gather_right(k))

    @pl.when(jnp.logical_not(mine))
    def _():
        push(*gather_right(0))

    @pl.when(mine)
    def _():
        rt[:, pl.ds(pl.multiple_of(block * rl, rl), rl), :] = rown[...]

    g_in.wait()
    obacc[...] = jnp.zeros_like(obacc)

    def back(k, _):
        rows = g[pl.ds(pl.multiple_of(k * 2 * nj, 2 * nj), 2 * nj), :]
        y = mm(wp[...], rows, NT_DIMS).astype(BF16)
        for q in range(2):
            at = pl.ds(pl.multiple_of((2 * k + q) * CH, CH), CH)
            for d in range(CH):
                pair[at, d * nj : (d + 1) * nj] = y[d * CH : (d + 1) * CH, q * nj : (q + 1) * nj]
        obacc[...] += jnp.sum(rows.astype(F32).reshape(2 * nj // 8, 8, CZ), 0)
        return 0

    lax.fori_loop(0, ni // 2, back, 0)

    for k in range(1, nc):
        arrived(*gather_left_in(k))

    def flip(k, _):
        at = pl.ds(pl.multiple_of(k * 128, 128), 128)
        lmat[:, at] = lt[at, :].T
        return 0

    lax.fori_loop(0, ni * CH // 128, flip, 0)

    def right_step(k, _):
        lanes = pl.ds(pl.multiple_of(k * 2 * nj, 2 * nj), 2 * nj)
        y = mm(lmat[...], pair[:, lanes]).T
        rp[pl.ds(2 * k, 2)] = y.reshape(2, nj, S).astype(BF16)
        return 0

    lax.fori_loop(0, CH // 2, right_step, 0)

    def scatter_right(k):
        where = {"row": rpc * c + k // nc, "col": k % nc}
        return rp.at[:, pl.ds(k * rl, rl), :], rr.at[r], sr_send.at[k], sr_recv.at[r], where

    def scatter_right_in(k):
        q = lax.rem(r + k, nr)
        where = {"row": q, "col": home}
        return rp.at[:, pl.ds(0, rl), :], rr.at[q], sr_send.at[0], sr_recv.at[q], where

    for k in range(nr):
        own = jnp.logical_and(mine, block == k)

        @pl.when(jnp.logical_not(own))
        def _():
            push(*scatter_right(k))

        @pl.when(own)
        def _():
            rr[r] = rp[:, k * rl : (k + 1) * rl, :]

    for k in range(nr):
        own = jnp.logical_and(mine, block == k)

        @pl.when(jnp.logical_not(own))
        def _():
            arrived(*gather_right_in(k))

    def left_rows(k):
        return pl.ds(pl.multiple_of(k * lrows, lrows), lrows)

    def scatter_left(k):
        q = lax.rem(c + k, nc)
        return lp.at[k], lr.at[c], sl_send.at[k], sl_recv.at[c], {"col": q}

    def scatter_left_in(k):
        q = lax.rem(c + k, nc)
        return lp.at[k], lr.at[q], sl_send.at[k], sl_recv.at[q], {"col": q}

    for k in range(1, nc + 1):
        q = lax.rem(c + k, nc)
        right_all = rt[...].reshape(CH * nj, S)
        y = mm(pair[left_rows(q), :], right_all).astype(BF16)
        if k < nc:
            lp[k] = y
            push(*scatter_left(k))
        else:
            lr[c] = y

    dw[...] = jnp.zeros_like(dw)

    def weigh(k, _):
        rows = lt[pl.ds(pl.multiple_of(k * 8 * CH, 8 * CH), 8 * CH), :]
        for v in range(8):
            part = rt[v * 4 : (v + 1) * 4].reshape(4 * nj, S)
            y = mm(rows, part, NT_DIMS).astype(BF16)
            for q in range(8):
                for d in range(4):
                    on[(v * 4 + d) * CH : (v * 4 + d + 1) * CH, q * nj : (q + 1) * nj] = y[
                        q * CH : (q + 1) * CH, d * nj : (d + 1) * nj
                    ]
        dw[...] += mm(on[...], g[pl.ds(pl.multiple_of(k * 8 * nj, 8 * nj), 8 * nj), :])
        return 0

    lax.fori_loop(0, ni // 8, weigh, 0)

    ar = CH * CH // nr
    ac = ar // nc

    def a_row(k):
        q = lax.rem(r + k, nr)
        src = dw.at[pl.ds(pl.multiple_of(q * ar, ar), ar), :]
        return src, a1.at[r], a_row_send.at[k], a_row_recv.at[r], {"row": q}

    def a_row_in(k):
        q = lax.rem(r + k, nr)
        src = dw.at[pl.ds(0, ar), :]
        return src, a1.at[q], a_row_send.at[k], a_row_recv.at[q], {"row": q}

    for k in range(1, nr):
        push(*a_row(k))
    a1[r] = dw[pl.ds(pl.multiple_of(r * ar, ar), ar), :]

    for k in range(1, nc):
        arrived(*scatter_left_in(k))
    for k in range(1, nr):
        arrived(*scatter_right_in(k))

    @pl.when(jnp.logical_not(mine))
    def _():
        arrived(*scatter_right_in(0))

    def sum_left(k, _):
        at = pl.ds(pl.multiple_of(k * 128, 128), 128)
        total = lr[0, at, :].astype(F32)
        for q in range(1, nc):
            total += lr[q, at, :].astype(F32)
        side[at, :] = total * (1.0 / S)
        return 0

    lax.fori_loop(0, lrows // 128, sum_left, 0)

    def sum_right(k, _):
        at = pl.ds(k * 8, 8)
        total = rr[0, at].astype(F32)
        for q in range(1, nr):
            total += rr[q, at].astype(F32)
        to = pl.ds(pl.multiple_of(lrows + k * 8 * rl, 8 * rl), 8 * rl)
        side[to, :] = total.reshape(8 * rl, S) * (1.0 / S)
        return 0

    lax.fori_loop(0, CH // 8, sum_right, 0)

    for k in range(1, nr):
        arrived(*a_row_in(k))
    total = a1[0]
    for q in range(1, nr):
        total += a1[q]
    s1[...] = total

    def a_col(k):
        q = lax.rem(c + k, nc)
        src = s1.at[pl.ds(pl.multiple_of(q * ac, ac), ac), :]
        return src, a2.at[c], a_col_send.at[k], a_col_recv.at[c], {"col": q}

    def a_col_in(k):
        q = lax.rem(c + k, nc)
        return s1.at[pl.ds(0, ac), :], a2.at[q], a_col_send.at[k], a_col_recv.at[q], {"col": q}

    for k in range(1, nc):
        push(*a_col(k))
    a2[c] = s1[pl.ds(pl.multiple_of(c * ac, ac), ac), :]

    pwt[...] = jnp.zeros_like(pwt)
    acc[...] = jnp.zeros_like(acc)

    def finish(k, _):
        left = side[pl.ds(pl.multiple_of(k * CH, CH), CH), :]
        right = side[pl.ds(lrows + k, CH, stride=rl), :]
        both = jnp.concatenate([left, right], 0)
        rounded = both.astype(BF16)
        turned = both.T
        acc[:, 2 * CM : 2 * CM + 2 * CH] += jnp.sum(turned.reshape(S // 8, 8, 2 * CH), 0)
        grad = mm(turned.astype(BF16), pt)
        pwt[...] += mm(rounded, no[pl.ds(pl.multiple_of(k * S, S), S), :])
        at = pl.ds(k, S, stride=rl)
        x = jnp.concatenate([nrm[0, at, :], nrm[1, at, :]], 1)
        scale = inv[at, :]
        acc[:, :CM] += jnp.sum((grad * x).reshape(S // 8, 8, CM), 0)
        acc[:, CM : 2 * CM] += jnp.sum(grad.reshape(S // 8, 8, CM), 0)
        scaled = grad * mult
        dx = scaled - jnp.mean(scaled, -1, keepdims=True) - x * jnp.mean(scaled * x, -1, keepdims=True)
        nrm[0, at, :] = dx[:, :128] * scale
        nrm[1, at, :] = dx[:, 128:] * scale
        return 0

    lax.fori_loop(0, rl, finish, 0)

    pr = 2 * 2 * CH // nr
    vr = 8 // nr
    vec[...] = jnp.zeros_like(vec)
    small = jnp.sum(acc[...], 0, keepdims=True)
    vec[0:1, : 2 * CH] = small[:, 2 * CM : 2 * CM + 2 * CH]
    for k in range(4):
        vec[1 + k : 2 + k, :] = small[:, k * 128 : (k + 1) * 128]
    vec[5:6, :] = jnp.sum(obacc[...], 0, keepdims=True)
    weights = pwt[...]
    stacked = jnp.concatenate([weights[:, :128], weights[:, 128:]], 0)
    sb[...] = jnp.zeros_like(sb)
    for q in range(nr):
        sb[q, :pr, :] = stacked[q * pr : (q + 1) * pr]
        sb[q, pr : pr + vr, :] = vec[q * vr : (q + 1) * vr, :]

    def b_row(k):
        q = lax.rem(r + k, nr)
        return sb.at[q], b1.at[r], b_row_send.at[k], b_row_recv.at[r], {"row": q}

    def b_row_in(k):
        q = lax.rem(r + k, nr)
        return sb.at[q], b1.at[q], b_row_send.at[k], b_row_recv.at[q], {"row": q}

    for k in range(1, nr):
        push(*b_row(k))
    b1[r] = sb[r]

    for k in range(1, nc):
        arrived(*a_col_in(k))
    total = a2[0]
    for q in range(1, nc):
        total += a2[q]
    a3[t] = total

    def a_tgt(k):
        q = lax.rem(t + k, nt)
        return a3.at[t], a3.at[t], a_tgt_send.at[k], a_tgt_recv.at[t], {"tgt": q}

    def a_tgt_in(k):
        q = lax.rem(t + k, nt)
        return a3.at[q], a3.at[q], a_tgt_send.at[k], a_tgt_recv.at[q], {"tgt": q}

    for k in range(1, nt):
        push(*a_tgt(k))

    def emit(k, _):
        rows = pl.ds(pl.multiple_of(k * 128, 128), 128)
        h[rows, :128] = nrm[0, rows, :].astype(BF16)
        h[rows, 128:] = nrm[1, rows, :].astype(BF16)
        return 0

    lax.fori_loop(0, S * rl // 128, emit, 0)
    dx_copy = pltpu.make_async_copy(h, dx_out, local_sem.at[2])
    dx_copy.start()

    for k in range(1, nr):
        arrived(*b_row_in(k))
    total = b1[0]
    for q in range(1, nr):
        total += b1[q]
    b2[c] = total

    def b_col(k):
        q = lax.rem(c + k, nc)
        return b2.at[c], b2.at[c], b_col_send.at[k], b_col_recv.at[c], {"col": q}

    def b_col_in(k):
        q = lax.rem(c + k, nc)
        return b2.at[q], b2.at[q], b_col_send.at[k], b_col_recv.at[q], {"col": q}

    for k in range(1, nc):
        push(*b_col(k))

    for k in range(1, nt):
        arrived(*a_tgt_in(k))
    total = a3[0]
    for q in range(1, nt):
        total += a3[q]
    a4[c] = total

    def a_col2(k):
        q = lax.rem(c + k, nc)
        return a4.at[c], a4.at[c], a_col2_send.at[k], a_col2_recv.at[c], {"col": q}

    def a_col2_in(k):
        q = lax.rem(c + k, nc)
        return a4.at[q], a4.at[q], a_col2_send.at[k], a_col2_recv.at[q], {"col": q}

    for k in range(1, nc):
        push(*a_col2(k))

    for k in range(1, nc):
        arrived(*b_col_in(k))
    total = b2[0]
    for q in range(1, nc):
        total += b2[q]
    b3[t] = total

    def b_tgt(k):
        q = lax.rem(t + k, nt)
        return b3.at[t], b3.at[t], b_tgt_send.at[k], b_tgt_recv.at[t], {"tgt": q}

    def b_tgt_in(k):
        q = lax.rem(t + k, nt)
        return b3.at[q], b3.at[q], b_tgt_send.at[k], b_tgt_recv.at[q], {"tgt": q}

    for k in range(1, nt):
        push(*b_tgt(k))

    for k in range(1, nc):
        arrived(*a_col2_in(k))
    a5[r] = a4[...].reshape(ar, CZ)

    def a_row2(k):
        q = lax.rem(r + k, nr)
        return a5.at[r], a5.at[r], a_row2_send.at[k], a_row2_recv.at[r], {"row": q}

    def a_row2_in(k):
        q = lax.rem(r + k, nr)
        return a5.at[q], a5.at[q], a_row2_send.at[k], a_row2_recv.at[q], {"row": q}

    for k in range(1, nr):
        push(*a_row2(k))

    for k in range(1, nt):
        arrived(*b_tgt_in(k))
    total = b3[0]
    for q in range(1, nt):
        total += b3[q]
    b4[r] = total

    def b_row2(k):
        q = lax.rem(r + k, nr)
        return b4.at[r], b4.at[r], b_row2_send.at[k], b_row2_recv.at[r], {"row": q}

    def b_row2_in(k):
        q = lax.rem(r + k, nr)
        return b4.at[q], b4.at[q], b_row2_send.at[k], b_row2_recv.at[q], {"row": q}

    for k in range(1, nr):
        push(*b_row2(k))

    factor = 1.0 / (nt * nr * nc * rl)
    for k in range(1, nr):
        arrived(*a_row2_in(k))

    def place(d, _):
        at = pl.multiple_of(d * CH, CH)
        rows = a5[lax.div(at, ar), pl.ds(pl.multiple_of(lax.rem(at, ar), CH), CH), :]
        ow_out[pl.ds(d, CH, stride=CH), :] = rows * (factor / S)
        return 0

    lax.fori_loop(0, CH, place, 0)

    for k in range(1, nr):
        arrived(*b_row2_in(k))
    whole = b4[:, :pr, :].reshape(4 * CH, 128) * factor
    pw_out[:128, :] = whole[: 2 * CH].T
    pw_out[128:, :] = whole[2 * CH :].T
    for q in range(nr):
        vec[q * vr : (q + 1) * vr, :] = b4[q, pr : pr + vr, :] * factor
    pbias_out[...] = vec[0:1, : 2 * CH]
    gain_out[...] = jnp.concatenate([vec[1:2, :], vec[2:3, :]], 1)
    shift_out[...] = jnp.concatenate([vec[3:4, :], vec[4:5, :]], 1)
    ob_out[...] = vec[5:6, :]

    dx_copy.wait()
    for k in range(1, nc):
        sent(*gather_left(k))
        sent(*scatter_left(k))
        sent(*a_col(k))
        sent(*a_col2(k))
        sent(*b_col(k))
    for k in range(1, nr):
        sent(*gather_right(k))
        sent(*a_row(k))
        sent(*a_row2(k))
        sent(*b_row(k))
        sent(*b_row2(k))
    for k in range(1, nt):
        sent(*a_tgt(k))
        sent(*b_tgt(k))

    @pl.when(jnp.logical_not(mine))
    def _():
        sent(*gather_right(0))

    for k in range(nr):
        own = jnp.logical_and(mine, block == k)

        @pl.when(jnp.logical_not(own))
        def _():
            sent(*scatter_right(k))


def per_device(
    homolog_activation_matrix,
    standardizer_multiplier,
    standardizer_offset,
    side_mapping_matrices,
    side_mapping_offsets,
    final_channel_matrix,
    residue_couple_cotangent,
):
    nt, nr, nc = axis_sizes()
    rl = homolog_activation_matrix.shape[2]
    ni, nj = rl * nc, rl * nr
    ar = CH * CH // nr
    pr = 4 * CH // nr + 8
    vmem = functools.partial(pl.BlockSpec, memory_space=pltpu.VMEM)
    hbm = functools.partial(pl.BlockSpec, memory_space=pl.ANY)

    def sems(n):
        return [pltpu.SemaphoreType.DMA((n,)), pltpu.SemaphoreType.DMA((n,))]

    results = pl.pallas_call(
        functools.partial(kernel, (nt, nr, nc, rl)),
        out_shape=(
            jax.ShapeDtypeStruct((S * rl, CM), BF16),
            jax.ShapeDtypeStruct((CM, 2 * CH), F32),
            jax.ShapeDtypeStruct((1, 2 * CH), F32),
            jax.ShapeDtypeStruct((1, CM), F32),
            jax.ShapeDtypeStruct((1, CM), F32),
            jax.ShapeDtypeStruct((CH * CH, CZ), F32),
            jax.ShapeDtypeStruct((1, CZ), F32),
        ),
        in_specs=[hbm(), vmem(), vmem(), vmem(), vmem(), vmem(), hbm()],
        out_specs=(hbm(), vmem(), vmem(), vmem(), vmem(), vmem(), vmem()),
        scratch_shapes=[
            pltpu.VMEM((S * rl, CM), BF16),
            pltpu.VMEM((ni * nj, CZ), BF16),
            pltpu.VMEM((2, S * rl, 128), F32),
            pltpu.VMEM((S * rl, 128), F32),
            pltpu.VMEM((S * rl, CM), BF16),
            pltpu.VMEM((ni * CH, S), BF16),
            pltpu.VMEM((S, ni * CH), BF16),
            pltpu.VMEM((CH, nj, S), BF16),
            pltpu.VMEM((CH, rl, S), BF16),
            pltpu.VMEM((rl * CH, S), F32),
            pltpu.VMEM((CH * CH, CZ), F32),
            pltpu.VMEM((CH * CH, CZ), BF16),
            pltpu.VMEM((ni * CH, CH * nj), BF16),
            pltpu.VMEM((CH, nj, S), BF16),
            pltpu.VMEM((nc, rl * CH, S), BF16),
            pltpu.VMEM((nr, CH, rl, S), BF16),
            pltpu.VMEM((nc, rl * CH, S), BF16),
            pltpu.VMEM((2 * rl * CH, S), F32),
            pltpu.VMEM((CH * CH, 8 * nj), BF16),
            pltpu.VMEM((CH * CH, CZ), F32),
            pltpu.VMEM((8, CZ), F32),
            pltpu.VMEM((nr, ar, CZ), F32),
            pltpu.VMEM((ar, CZ), F32),
            pltpu.VMEM((nc, ar // nc, CZ), F32),
            pltpu.VMEM((nt, ar // nc, CZ), F32),
            pltpu.VMEM((nc, ar // nc, CZ), F32),
            pltpu.VMEM((nr, ar, CZ), F32),
            pltpu.VMEM((2 * CH, CM), F32),
            pltpu.VMEM((8, 128), F32),
            pltpu.VMEM((8, 2 * CM + 128), F32),
            pltpu.VMEM((nr, pr, 128), F32),
            pltpu.VMEM((nr, pr, 128), F32),
            pltpu.VMEM((nc, pr, 128), F32),
            pltpu.VMEM((nt, pr, 128), F32),
            pltpu.VMEM((nr, pr, 128), F32),
            pltpu.SemaphoreType.DMA((3,)),
        ]
        + sems(nc)
        + sems(nr)
        + sems(nc)
        + sems(nr)
        + sems(nr)
        + sems(nc)
        + sems(nt)
        + sems(nc)
        + sems(nr)
        + sems(nr)
        + sems(nc)
        + sems(nt)
        + sems(nr),
        compiler_params=pltpu.CompilerParams(
            collective_id=0, has_side_effects=True, vmem_limit_bytes=56 * 1024 * 1024
        ),
        cost_estimate=pl.CostEstimate(
            flops=10 * ni * nj * CH * CH * CZ, bytes_accessed=5 * 1024 * 1024, transcendentals=0
        ),
    )(
        homolog_activation_matrix.reshape(S * rl, CM),
        standardizer_multiplier.reshape(1, CM),
        standardizer_offset.reshape(1, CM),
        side_mapping_matrices,
        side_mapping_offsets.reshape(1, 2 * CH),
        final_channel_matrix,
        residue_couple_cotangent.reshape(ni * nj, CZ),
    )
    return (
        results[0].reshape(1, S, rl, CM),
        results[1],
        results[2].reshape(2 * CH),
        results[3].reshape(CM),
        results[4].reshape(CM),
        results[5],
        results[6].reshape(CZ),
    )


def solution(mesh):
    placed = (
        P("tgt", None, ("row", "col"), None),
        P(),
        P(),
        P(),
        P(),
        P(),
        P("tgt", "row", "col", None),
    )
    return jax.shard_map(
        per_device,
        mesh=mesh,
        in_specs=placed,
        out_specs=(P("tgt", None, ("row", "col"), None), P(), P(), P(), P(), P(), P()),
        check_vma=False,
    )
```

time: 866 us -> 133 us (0.15)
  waiting for transfers between devices: 572 us -> 0 us
  Pallas kernels: 0 us -> 123 us
  blocking collectives: 123 us -> 0 us
  matrix products: 66.6 us -> 0 us
  local copies, waits for them, and re-layouts: 69.8 us -> 8.39 us
  between operations: 14 us -> 0.69 us
  other arithmetic: 10.9 us -> 0 us
    all_gather x1 -> x0, waiting for transfers between devices: 205 us -> none  [per_device(): lax.all_gather(projected[..., CH:], ('row', 'col'), axis=1, tiled=True)]
    reduce_scatter x2 -> x0, waiting for transfers between devices: 197 us -> none  [the longest x1 162 us: per_device(): lax.psum_scatter(embedded, ('row', 'col'), scatter_dimension=1, tiled=True)]
    psum x1 -> x0, waiting for transfers between devices: 170 us -> none  [per_device(): lax.psum((addend_contributions[0], addend_contributions[1], addend_contri...]
    pallas_call x0 -> x1, Pallas kernels: none -> 123 us  [per_device(): pl.pallas_call(functools.partial(kernel, (nt, nr, nc, rl)), out_shape=(ja...]
    psum x1 -> x0, blocking collectives: 96.5 us -> none  [per_device(): lax.psum((addend_contributions[0], addend_contributions[1], addend_contri...]
    dot_general x23 -> x0, matrix products: 66.6 us -> none  [the longest x4 16.9 us: block_step(): jnp.einsum('ije,ke->ijk', grad_block, final_channel_matrix, preferred_ele...]
    convert_element_type x10 -> x0, local copies, waits for them, and re-layouts: 34.1 us -> none  [the longest x4 25.6 us: block_step(): pair_back.astype(jnp.bfloat16).reshape(block_rows, cols_here, CH, CH)]
    all_gather x1 -> x0, blocking collectives: 26.3 us -> none  [per_device(): left_panel = lax.all_gather(projected[..., :CH], 'col', axis=1, tiled=True)]
  transfers between devices with their start and end apart: 4 -> 0, of which waited for: 4 -> 0; matrix products, arithmetic and copies ran while one was open for 2% -> 0% of each run, Pallas kernels for 0% -> 0%
where the time goes in v1:
time: 133 us; the launch traced here: 132 us
  Pallas kernels  123 us (92%)
  local copies, waits for them, and re-layouts  8.39 us (6%)
    pallas_call x1, Pallas kernels, per_device(): pl.pallas_call(functools.partial(kernel, (nt, nr, nc, rl)), out_shape=(ja...  123 us
    unnamed x18, local copies, waits for them, and re-layouts  8.39 us

profile of v1, /device:TPU:1, one launch (start us, length us, event | category | flops | bytes accessed | tf_op | source)
XLA Modules:
  0.0 132.4 jit_solution(17096892471439993547)
XLA Ops:
  0.6 1.5 %copy.14.pm_ref = bf16[256,64]{1,0:T(8,128)(2,1)} copy(bf16[256,64]{0,1:T(8,128)(2,1)} %param.10) | data formatting | bytes 65536 | tf_op args[3]
  2.1 123.3 %shard_map.126 = (bf16[2048,256]{1,0:T(8,128)(2,1)}, f32[256,64]{1,0:T(8,128)}, f32[1,64]{1,0:T(1,128)}, f32[1,256]{1,0:T(1,128)}, f32[1,256]{1,0:T(1,128)}, /*index=5*/f32[1024,128]{1,0:T(8,128)}, f32[1,128]{1,0:T(1,128)}) custom-call(bf16[2048,256]{1,0:T(8,128)(2,1)} %bitcast.14, f32[1,256]{1,0:T(1,128)} %bitcast.15, f32[1,256]{1,0:T(1,128)} %bitcast.16, ...), custom_call_target="tpu_custom_call" | custom-call | flops 10737418240 | bytes 5242880 | tf_op jit(solution)/shard_map/pallas_call | solution.py:662
  125.5 0.0 copy-start.4
  125.5 0.0 copy-start.2
  125.5 0.0 copy-start.1
  125.5 0.0 copy-start
  125.5 0.0 copy-start.3
  125.5 1.7 %copy.15 = f32[256,64]{0,1:T(8,128)} copy(f32[256,64]{1,0:T(8,128)} %get-tuple-element.22) | data formatting | bytes 131072
  127.2 2.3 %copy.22 = bf16[1,128,16,256]{3,2,1,0:T(8,128)(2,1)} copy(bf16[1,128,16,256]{3,2,1,0:T(8,128)(2,1)} %bitcast.10) | data formatting | bytes 2097152
  129.5 0.0 copy-done.4
  129.5 0.5 copy.23
  130.0 0.0 copy-done.2
  130.0 0.6 copy.24
  130.5 0.0 copy-done.1
  130.5 0.6 copy.25
  131.1 0.0 copy-done
  131.1 0.8 copy.26
  131.9 0.0 copy-done.3
  131.9 0.5 copy.27
Async XLA Ops:
  125.5 4.0 %copy-start.4 = (f32[1,64]{1,0:T(1,128)S(1)}, f32[1,64]{1,0:T(1,128)}, u32[]{:S(2)}) copy-start(f32[1,64]{1,0:T(1,128)} %get-tuple-element.16) | copy-start | bytes 772
  125.5 4.5 %copy-start.2 = (f32[1,256]{1,0:T(1,128)S(1)}, f32[1,256]{1,0:T(1,128)}, u32[]{:S(2)}) copy-start(f32[1,256]{1,0:T(1,128)} %get-tuple-element.17) | copy-start | bytes 3076
  125.5 5.0 %copy-start.1 = (f32[1,256]{1,0:T(1,128)S(1)}, f32[1,256]{1,0:T(1,128)}, u32[]{:S(2)}) copy-start(f32[1,256]{1,0:T(1,128)} %get-tuple-element.18) | copy-start | bytes 3076
  125.5 5.6 %copy-start = (f32[1024,128]{1,0:T(8,128)S(1)}, f32[1024,128]{1,0:T(8,128)}, u32[]{:S(2)}) copy-start(f32[1024,128]{1,0:T(8,128)} %get-tuple-element.40) | copy-start | bytes 1572868
  125.5 6.4 %copy-start.3 = (f32[1,128]{1,0:T(1,128)S(1)}, f32[1,128]{1,0:T(1,128)}, u32[]{:S(2)}) copy-start(f32[1,128]{1,0:T(1,128)} %get-tuple-element.20) | copy-start | bytes 1540

commit v2 on v1

--- a/solution.py
+++ b/solution.py
@@ -107,11 +107,16 @@
     pair,
     rp,
     lp,
+    ra,
+    rb,
+    ms,
     rr,
-    lr,
+    la,
+    lb,
     side,
     on,
     dw,
+    dwb,
     obacc,
     a1,
     s1,
@@ -130,12 +135,24 @@
     local_sem,
     gl_send,
     gl_recv,
+    gl2_send,
+    gl2_recv,
+    gr1_send,
+    gr1_recv,
     gr_send,
     gr_recv,
-    sl_send,
-    sl_recv,
-    sr_send,
-    sr_recv,
+    gr2_send,
+    gr2_recv,
+    sr1_send,
+    sr1_recv,
+    sr2_send,
+    sr2_recv,
+    sr3_send,
+    sr3_recv,
+    sl1_send,
+    sl1_recv,
+    sl2_send,
+    sl2_recv,
     a_row_send,
     a_row_recv,
     a_col_send,
@@ -157,12 +174,15 @@
 ):
     nt, nr, nc, rl = sizes
     rpc = nr // nc
+    nx = nr // rpc
+    assert nx == nc == 4 and rpc == 2
     ni, nj = rl * nc, rl * nr
     lrows = rl * CH
     t, r, c = axis_places()
     home = lax.div(r, rpc)
-    block = lax.rem(r, rpc) * nc + c
-    mine = c == home
+    z, x_at, q_at = lax.div(r, nx), lax.rem(r, nx), lax.rem(r, rpc)
+    own = jnp.logical_and(x_at == c, home == c)
+    half, lhalf = CH // 2, lrows // 2
 
     h_in = pltpu.make_async_copy(h_ref, h, local_sem.at[0])
     h_in.start()
@@ -172,8 +192,7 @@
 
     mult = mult_ref[...]
     off = off_ref[...]
-    pt32 = pm_ref[...].astype(F32).T
-    pt = pt32.astype(BF16)
+    pt = pm_ref[...]
     bias = jnp.broadcast_to(pb_ref[...], (S, 2 * CH)).T
 
     wf[...] = w_ref[...].astype(F32)
@@ -218,41 +237,81 @@
     lax.fori_loop(0, CH, turn, 0)
     meet(nt, nr, nc)
 
-    def left_block(k):
-        return lt.at[pl.ds(pl.multiple_of(k * lrows, lrows), lrows), :]
-
-    def right_block(k):
-        return rt.at[:, pl.ds(pl.multiple_of(k * rl, rl), rl), :]
+    def xs(k):
+        return lax.rem(x_at + k, nx)
+
+    def cs(k):
+        return lax.rem(c + k, nc)
+
+    def to_x(k):
+        return {"row": z * nx + xs(1 if k == 0 else nx - 1)}
+
+    def to_c(k):
+        return {"col": cs(1 if k == 0 else nc - 1)}
+
+    back_of = (3, 1)
+
+    def left_block(k, part=None):
+        at, size = (k * lrows, lrows) if part is None else (k * lrows + part * lhalf, lhalf)
+        return lt.at[pl.ds(pl.multiple_of(at, lhalf), size), :]
+
+    def right_block(k, part=None):
+        at = pl.ds(pl.multiple_of(k * rl, rl), rl)
+        if part is None:
+            return rt.at[:, :, at, :]
+        return rt.at[part * half : (part + 1) * half, :, at, :]
 
     def gather_left(k):
-        q = lax.rem(c + k, nc)
-        return left_block(c), left_block(c), gl_send.at[k], gl_recv.at[c], {"col": q}
+        return left_block(c), left_block(c), gl_send.at[k], gl_recv.at[k], to_c(k)
 
     def gather_left_in(k):
-        q = lax.rem(c + k, nc)
-        return left_block(q), left_block(q), gl_send.at[k], gl_recv.at[q], {"col": q}
+        at = left_block(cs(back_of[k]))
+        return at, at, gl_send.at[k], gl_recv.at[k], to_c(k)
+
+    def relay_left(k):
+        at = left_block(cs(back_of[k]), k)
+        return at, at, gl2_send.at[k], gl2_recv.at[k], to_c(k)
+
+    def relay_left_in(k):
+        at = left_block(cs(2), k)
+        return at, at, gl2_send.at[k], gl2_recv.at[k], to_c(k)
+
+    def first_right(k):
+        to = rt.at[:, q_at, pl.ds(pl.multiple_of(c * rl, rl), rl), :]
+        return rown, to, gr1_send.at[k], gr1_recv.at[q_at], {"row": k * nx + c, "col": home}
+
+    def first_right_in(k):
+        to = rt.at[:, k, pl.ds(pl.multiple_of(x_at * rl, rl), rl), :]
+        return rown, to, gr1_send.at[k], gr1_recv.at[k], {"row": rpc * c + k, "col": x_at}
 
     def gather_right(k):
-        q = lax.rem(r + k, nr)
-        where = {"row": q, "col": home}
-        return rown, right_block(block), gr_send.at[k], gr_recv.at[block], where
+        at = right_block(x_at)
+        return at, at, gr_send.at[k], gr_recv.at[k], to_x(k)
 
     def gather_right_in(k):
-        where = {"row": rpc * c + k // nc, "col": k % nc}
-        return rown, right_block(k), gr_send.at[0], gr_recv.at[k], where
-
-    for k in range(1, nc):
+        at = right_block(xs(back_of[k]))
+        return at, at, gr_send.at[k], gr_recv.at[k], to_x(k)
+
+    def relay_right(k):
+        at = right_block(xs(back_of[k]), k)
+        return at, at, gr2_send.at[k], gr2_recv.at[k], to_x(k)
+
+    def relay_right_in(k):
+        at = right_block(xs(2), k)
+        return at, at, gr2_send.at[k], gr2_recv.at[k], to_x(k)
+
+    def unless(same, act):
+        pl.when(jnp.logical_not(jnp.logical_and(own, same)))(act)
+
+    for k in range(rpc):
+        unless(z == k, lambda: push(*first_right(k)))
+
+    @pl.when(own)
+    def _():
+        rt[:, q_at, pl.ds(pl.multiple_of(c * rl, rl), rl), :] = rown[...]
+
+    for k in range(2):
         push(*gather_left(k))
-    for k in range(1, nr):
-        push(*gather_right(k))
-
-    @pl.when(jnp.logical_not(mine))
-    def _():
-        push(*gather_right(0))
-
-    @pl.when(mine)
-    def _():
-        rt[:, pl.ds(pl.multiple_of(block * rl, rl), rl), :] = rown[...]
 
     g_in.wait()
     obacc[...] = jnp.zeros_like(obacc)
@@ -267,10 +326,23 @@
         obacc[...] += jnp.sum(rows.astype(F32).reshape(2 * nj // 8, 8, CZ), 0)
         return 0
 
-    lax.fori_loop(0, ni // 2, back, 0)
-
-    for k in range(1, nc):
+    lax.fori_loop(0, ni // 4, back, 0)
+    for k in range(rpc):
+        unless(q_at == k, lambda: arrived(*first_right_in(k)))
+    for k in range(2):
+        push(*gather_right(k))
+    for k in range(2):
         arrived(*gather_left_in(k))
+    for k in range(2):
+        push(*relay_left(k))
+    lax.fori_loop(ni // 4, ni // 2, back, 0)
+
+    for k in range(2):
+        arrived(*gather_right_in(k))
+    for k in range(2):
+        push(*relay_right(k))
+    for k in range(2):
+        arrived(*relay_left_in(k))
 
     def flip(k, _):
         at = pl.ds(pl.multiple_of(k * 128, 128), 128)
@@ -282,58 +354,72 @@
     def right_step(k, _):
         lanes = pl.ds(pl.multiple_of(k * 2 * nj, 2 * nj), 2 * nj)
         y = mm(lmat[...], pair[:, lanes]).T
-        rp[pl.ds(2 * k, 2)] = y.reshape(2, nj, S).astype(BF16)
+        rp[pl.ds(2 * k, 2)] = y.reshape(2, rpc, nj // rpc, S).astype(BF16)
         return 0
 
     lax.fori_loop(0, CH // 2, right_step, 0)
 
+    def right_sum(k, part=None):
+        at = pl.ds(pl.multiple_of(k * rl, rl), rl)
+        if part is None:
+            return rp.at[:, :, at, :]
+        return rp.at[part * half : (part + 1) * half, :, at, :]
+
+    def far_right(k):
+        return right_sum(xs(2), k), ra.at[k], sr1_send.at[k], sr1_recv.at[k], to_x(k)
+
+    def near_right(k):
+        at = right_sum(xs(1 if k == 0 else 3))
+        return at, rb.at[k], sr2_send.at[k], sr2_recv.at[k], to_x(k)
+
     def scatter_right(k):
-        where = {"row": rpc * c + k // nc, "col": k % nc}
-        return rp.at[:, pl.ds(k * rl, rl), :], rr.at[r], sr_send.at[k], sr_recv.at[r], where
+        where = {"row": rpc * c + k, "col": x_at}
+        return ms.at[k], rr.at[z], sr3_send.at[k], sr3_recv.at[z], where
 
     def scatter_right_in(k):
-        q = lax.rem(r + k, nr)
-        where = {"row": q, "col": home}
-        return rp.at[:, pl.ds(0, rl), :], rr.at[q], sr_send.at[0], sr_recv.at[q], where
-
-    for k in range(nr):
-        own = jnp.logical_and(mine, block == k)
-
-        @pl.when(jnp.logical_not(own))
-        def _():
-            push(*scatter_right(k))
-
-        @pl.when(own)
-        def _():
-            rr[r] = rp[:, k * rl : (k + 1) * rl, :]
-
-    for k in range(nr):
-        own = jnp.logical_and(mine, block == k)
-
-        @pl.when(jnp.logical_not(own))
-        def _():
-            arrived(*gather_right_in(k))
+        where = {"row": k * nx + c, "col": home}
+        return ms.at[k], rr.at[k], sr3_send.at[k], sr3_recv.at[k], where
+
+    for k in range(2):
+        push(*far_right(k))
+
+    for k in range(2):
+        arrived(*relay_right_in(k))
 
     def left_rows(k):
         return pl.ds(pl.multiple_of(k * lrows, lrows), lrows)
 
-    def scatter_left(k):
-        q = lax.rem(c + k, nc)
-        return lp.at[k], lr.at[c], sl_send.at[k], sl_recv.at[c], {"col": q}
-
-    def scatter_left_in(k):
-        q = lax.rem(c + k, nc)
-        return lp.at[k], lr.at[q], sl_send.at[k], sl_recv.at[q], {"col": q}
-
-    for k in range(1, nc + 1):
-        q = lax.rem(c + k, nc)
+    def far_left(k):
+        at = lp.at[cs(2), k * lhalf : (k + 1) * lhalf]
+        return at, la.at[k], sl1_send.at[k], sl1_recv.at[k], to_c(k)
+
+    def near_left(k):
+        at = lp.at[cs(1 if k == 0 else 3)]
+        return at, lb.at[k], sl2_send.at[k], sl2_recv.at[k], to_c(k)
+
+    def left_step(k, _):
         right_all = rt[...].reshape(CH * nj, S)
-        y = mm(pair[left_rows(q), :], right_all).astype(BF16)
-        if k < nc:
-            lp[k] = y
-            push(*scatter_left(k))
-        else:
-            lr[c] = y
+        lp[k] = mm(pair[left_rows(k), :], right_all).astype(BF16)
+        return 0
+
+    left_step(cs(2), 0)
+    for k in range(2):
+        push(*far_left(k))
+    left_step(cs(1), 0)
+    for k in range(2):
+        arrived(*far_right(k))
+    for k in range(2):
+        at = right_sum(xs(1 if k == 0 else 3), k)
+        at[...] = (at[...].astype(F32) + ra[k].astype(F32)).astype(BF16)
+        push(*near_right(k))
+    left_step(cs(3), 0)
+    for k in range(2):
+        arrived(*far_left(k))
+    for k in range(2):
+        at = lp.at[cs(1 if k == 0 else 3), k * lhalf : (k + 1) * lhalf]
+        at[...] = (at[...].astype(F32) + la[k].astype(F32)).astype(BF16)
+        push(*near_left(k))
+    left_step(c, 0)
 
     dw[...] = jnp.zeros_like(dw)
 
@@ -350,39 +436,52 @@
         dw[...] += mm(on[...], g[pl.ds(pl.multiple_of(k * 8 * nj, 8 * nj), 8 * nj), :])
         return 0
 
-    lax.fori_loop(0, ni // 8, weigh, 0)
+    lax.fori_loop(0, ni // 16, weigh, 0)
+    for k in range(2):
+        arrived(*near_right(k))
+    for k in range(rpc):
+        at = pl.ds(pl.multiple_of(x_at * rl, rl), rl)
+        total = rp[:, k, at, :].astype(F32)
+        total += rb[0, :, k].astype(F32)
+        total += rb[1, :, k].astype(F32)
+        ms[k] = total.astype(BF16)
+    for k in range(rpc):
+        unless(q_at == k, lambda: push(*scatter_right(k)))
+
+    @pl.when(own)
+    def _():
+        rr[z] = ms[q_at]
+
+    lax.fori_loop(ni // 16, ni // 8, weigh, 0)
 
     ar = CH * CH // nr
     ac = ar // nc
 
     def a_row(k):
         q = lax.rem(r + k, nr)
-        src = dw.at[pl.ds(pl.multiple_of(q * ar, ar), ar), :]
+        src = dwb.at[pl.ds(pl.multiple_of(q * ar, ar), ar), :]
         return src, a1.at[r], a_row_send.at[k], a_row_recv.at[r], {"row": q}
 
     def a_row_in(k):
         q = lax.rem(r + k, nr)
-        src = dw.at[pl.ds(0, ar), :]
+        src = dwb.at[pl.ds(0, ar), :]
         return src, a1.at[q], a_row_send.at[k], a_row_recv.at[q], {"row": q}
 
+    dwb[...] = dw[...].astype(BF16)
     for k in range(1, nr):
         push(*a_row(k))
-    a1[r] = dw[pl.ds(pl.multiple_of(r * ar, ar), ar), :]
-
-    for k in range(1, nc):
-        arrived(*scatter_left_in(k))
-    for k in range(1, nr):
-        arrived(*scatter_right_in(k))
-
-    @pl.when(jnp.logical_not(mine))
-    def _():
-        arrived(*scatter_right_in(0))
+    a1[r] = dwb[pl.ds(pl.multiple_of(r * ar, ar), ar), :]
+
+    for k in range(2):
+        arrived(*near_left(k))
+    for k in range(rpc):
+        unless(z == k, lambda: arrived(*scatter_right_in(k)))
 
     def sum_left(k, _):
         at = pl.ds(pl.multiple_of(k * 128, 128), 128)
-        total = lr[0, at, :].astype(F32)
-        for q in range(1, nc):
-            total += lr[q, at, :].astype(F32)
+        total = lp[c, at, :].astype(F32)
+        for q in range(2):
+            total += lb[q, at, :].astype(F32)
         side[at, :] = total * (1.0 / S)
         return 0
 
@@ -391,7 +490,7 @@
     def sum_right(k, _):
         at = pl.ds(k * 8, 8)
         total = rr[0, at].astype(F32)
-        for q in range(1, nr):
+        for q in range(1, rpc):
             total += rr[q, at].astype(F32)
         to = pl.ds(pl.multiple_of(lrows + k * 8 * rl, 8 * rl), 8 * rl)
         side[to, :] = total.reshape(8 * rl, S) * (1.0 / S)
@@ -401,9 +500,9 @@
 
     for k in range(1, nr):
         arrived(*a_row_in(k))
-    total = a1[0]
+    total = a1[0].astype(F32)
     for q in range(1, nr):
-        total += a1[q]
+        total += a1[q].astype(F32)
     s1[...] = total
 
     def a_col(k):
@@ -522,7 +621,7 @@
     total = a3[0]
     for q in range(1, nt):
         total += a3[q]
-    a4[c] = total
+    a4[c] = total.astype(BF16)
 
     def a_col2(k):
         q = lax.rem(c + k, nc)
@@ -593,7 +692,7 @@
     def place(d, _):
         at = pl.multiple_of(d * CH, CH)
         rows = a5[lax.div(at, ar), pl.ds(pl.multiple_of(lax.rem(at, ar), CH), CH), :]
-        ow_out[pl.ds(d, CH, stride=CH), :] = rows * (factor / S)
+        ow_out[pl.ds(d, CH, stride=CH), :] = rows.astype(F32) * (factor / S)
         return 0
 
     lax.fori_loop(0, CH, place, 0)
@@ -601,8 +700,8 @@
     for k in range(1, nr):
         arrived(*b_row2_in(k))
     whole = b4[:, :pr, :].reshape(4 * CH, 128) * factor
-    pw_out[:128, :] = whole[: 2 * CH].T
-    pw_out[128:, :] = whole[2 * CH :].T
+    pw_out[:, :128] = whole[: 2 * CH]
+    pw_out[:, 128:] = whole[2 * CH :]
     for q in range(nr):
         vec[q * vr : (q + 1) * vr, :] = b4[q, pr : pr + vr, :] * factor
     pbias_out[...] = vec[0:1, : 2 * CH]
@@ -611,14 +710,23 @@
     ob_out[...] = vec[5:6, :]
 
     dx_copy.wait()
+    for k in range(2):
+        sent(*gather_left(k))
+        sent(*relay_left(k))
+        sent(*gather_right(k))
+        sent(*relay_right(k))
+        sent(*far_right(k))
+        sent(*near_right(k))
+        sent(*far_left(k))
+        sent(*near_left(k))
+    for k in range(rpc):
+        unless(z == k, lambda: sent(*first_right(k)))
+        unless(q_at == k, lambda: sent(*scatter_right(k)))
     for k in range(1, nc):
-        sent(*gather_left(k))
-        sent(*scatter_left(k))
         sent(*a_col(k))
         sent(*a_col2(k))
         sent(*b_col(k))
     for k in range(1, nr):
-        sent(*gather_right(k))
         sent(*a_row(k))
         sent(*a_row2(k))
         sent(*b_row(k))
@@ -626,17 +734,6 @@
     for k in range(1, nt):
         sent(*a_tgt(k))
         sent(*b_tgt(k))
-
-    @pl.when(jnp.logical_not(mine))
-    def _():
-        sent(*gather_right(0))
-
-    for k in range(nr):
-        own = jnp.logical_and(mine, block == k)
-
-        @pl.when(jnp.logical_not(own))
-        def _():
-            sent(*scatter_right(k))
 
 
 def per_device(
@@ -663,7 +760,7 @@
         functools.partial(kernel, (nt, nr, nc, rl)),
         out_shape=(
             jax.ShapeDtypeStruct((S * rl, CM), BF16),
-            jax.ShapeDtypeStruct((CM, 2 * CH), F32),
+            jax.ShapeDtypeStruct((2 * CH, CM), F32),
             jax.ShapeDtypeStruct((1, 2 * CH), F32),
             jax.ShapeDtypeStruct((1, CM), F32),
             jax.ShapeDtypeStruct((1, CM), F32),
@@ -680,26 +777,31 @@
             pltpu.VMEM((S * rl, CM), BF16),
             pltpu.VMEM((ni * CH, S), BF16),
             pltpu.VMEM((S, ni * CH), BF16),
-            pltpu.VMEM((CH, nj, S), BF16),
+            pltpu.VMEM((CH, 2, nj // 2, S), BF16),
             pltpu.VMEM((CH, rl, S), BF16),
             pltpu.VMEM((rl * CH, S), F32),
             pltpu.VMEM((CH * CH, CZ), F32),
             pltpu.VMEM((CH * CH, CZ), BF16),
             pltpu.VMEM((ni * CH, CH * nj), BF16),
-            pltpu.VMEM((CH, nj, S), BF16),
+            pltpu.VMEM((CH, 2, nj // 2, S), BF16),
             pltpu.VMEM((nc, rl * CH, S), BF16),
-            pltpu.VMEM((nr, CH, rl, S), BF16),
-            pltpu.VMEM((nc, rl * CH, S), BF16),
+            pltpu.VMEM((2, CH // 2, 2, rl, S), BF16),
+            pltpu.VMEM((2, CH, 2, rl, S), BF16),
+            pltpu.VMEM((2, CH, rl, S), BF16),
+            pltpu.VMEM((2, CH, rl, S), BF16),
+            pltpu.VMEM((2, rl * CH // 2, S), BF16),
+            pltpu.VMEM((2, rl * CH, S), BF16),
             pltpu.VMEM((2 * rl * CH, S), F32),
             pltpu.VMEM((CH * CH, 8 * nj), BF16),
             pltpu.VMEM((CH * CH, CZ), F32),
+            pltpu.VMEM((CH * CH, CZ), BF16),
             pltpu.VMEM((8, CZ), F32),
-            pltpu.VMEM((nr, ar, CZ), F32),
+            pltpu.VMEM((nr, ar, CZ), BF16),
             pltpu.VMEM((ar, CZ), F32),
             pltpu.VMEM((nc, ar // nc, CZ), F32),
             pltpu.VMEM((nt, ar // nc, CZ), F32),
-            pltpu.VMEM((nc, ar // nc, CZ), F32),
-            pltpu.VMEM((nr, ar, CZ), F32),
+            pltpu.VMEM((nc, ar // nc, CZ), BF16),
+            pltpu.VMEM((nr, ar, CZ), BF16),
             pltpu.VMEM((2 * CH, CM), F32),
             pltpu.VMEM((8, 128), F32),
             pltpu.VMEM((8, 2 * CM + 128), F32),
@@ -710,10 +812,7 @@
             pltpu.VMEM((nr, pr, 128), F32),
             pltpu.SemaphoreType.DMA((3,)),
         ]
-        + sems(nc)
-        + sems(nr)
-        + sems(nc)
-        + sems(nr)
+        + 10 * sems(2)
         + sems(nr)
         + sems(nc)
         + sems(nt)
@@ -733,14 +832,14 @@
         homolog_activation_matrix.reshape(S * rl, CM),
         standardizer_multiplier.reshape(1, CM),
         standardizer_offset.reshape(1, CM),
-        side_mapping_matrices,
+        side_mapping_matrices.T,
         side_mapping_offsets.reshape(1, 2 * CH),
         final_channel_matrix,
         residue_couple_cotangent.reshape(ni * nj, CZ),
     )
     return (
         results[0].reshape(1, S, rl, CM),
-        results[1],
+        results[1].T,
         results[2].reshape(2 * CH),
         results[3].reshape(CM),
         results[4].reshape(CM),

time: 133 us -> 108 us (0.81)
  Pallas kernels: 123 us -> 101 us
  local copies, waits for them, and re-layouts: 8.39 us -> 5.92 us
    pallas_call x1, Pallas kernels: 123 us -> 101 us  [per_device(): pl.pallas_call(functools.partial(kernel, (nt, nr, nc, rl)), out_shape=(ja...]
    unnamed x18 -> x19, local copies, waits for them, and re-layouts: 8.39 us -> 5.92 us
where the time goes in v2:
time: 108 us
  Pallas kernels  101 us (94%)
  local copies, waits for them, and re-layouts  5.92 us (5%)
    pallas_call x1, Pallas kernels, per_device(): pl.pallas_call(functools.partial(kernel, (nt, nr, nc, rl)), out_shape=(ja...  101 us
    unnamed x19, local copies, waits for them, and re-layouts  5.92 us

profile of v2, /device:TPU:1, one launch (start us, length us, event | category | flops | bytes accessed | tf_op | source)
XLA Modules:
  0.0 108.0 jit_solution(2868836254768844597)
XLA Ops:
  0.6 101.3 %shard_map.126 = (bf16[2048,256]{1,0:T(8,128)(2,1)}, f32[64,256]{1,0:T(8,128)}, f32[1,64]{1,0:T(1,128)}, f32[1,256]{1,0:T(1,128)}, f32[1,256]{1,0:T(1,128)}, /*index=5*/f32[1024,128]{1,0:T(8,128)}, f32[1,128]{1,0:T(1,128)}) custom-call(bf16[2048,256]{1,0:T(8,128)(2,1)} %bitcast.17, f32[1,256]{1,0:T(1,128)} %bitcast.19, f32[1,256]{1,0:T(1,128)} %bitcast.20, ...), custom_call_target="tpu_custom_call" | custom-call | flops 10737418240 | bytes 5242880 | tf_op jit(solution)/shard_map/pallas_call | solution.py:759
  102.0 0.0 copy-start.1
  102.0 0.0 copy-start.5
  102.0 0.0 copy-start.3
  102.0 0.0 copy-start.2
  102.0 0.0 copy-start
  102.0 0.0 copy-start.4
  102.0 2.3 %copy.21 = bf16[1,128,16,256]{3,2,1,0:T(8,128)(2,1)} copy(bf16[1,128,16,256]{3,2,1,0:T(8,128)(2,1)} %bitcast.12) | data formatting | bytes 2097152
  104.4 0.0 copy-done.1
  104.4 0.6 copy.22
  105.0 0.0 copy-done.5
  105.0 0.5 copy.23
  105.5 0.0 copy-done.3
  105.5 0.6 copy.24
  106.1 0.0 copy-done.2
  106.1 0.6 copy.25
  106.6 0.0 copy-done
  106.7 0.8 copy.26
  107.4 0.0 copy-done.4
  107.4 0.5 copy.27
Async XLA Ops:
  102.0 2.4 %copy-start.1 = (f32[64,256]{1,0:T(8,128)S(1)}, f32[64,256]{1,0:T(8,128)}, u32[]{:S(2)}) copy-start(f32[64,256]{1,0:T(8,128)} %get-tuple-element.15) | copy-start | bytes 196612
  102.0 3.0 %copy-start.5 = (f32[1,64]{1,0:T(1,128)S(1)}, f32[1,64]{1,0:T(1,128)}, u32[]{:S(2)}) copy-start(f32[1,64]{1,0:T(1,128)} %get-tuple-element.16) | copy-start | bytes 772
  102.0 3.5 %copy-start.3 = (f32[1,256]{1,0:T(1,128)S(1)}, f32[1,256]{1,0:T(1,128)}, u32[]{:S(2)}) copy-start(f32[1,256]{1,0:T(1,128)} %get-tuple-element.17) | copy-start | bytes 3076
  102.0 4.1 %copy-start.2 = (f32[1,256]{1,0:T(1,128)S(1)}, f32[1,256]{1,0:T(1,128)}, u32[]{:S(2)}) copy-start(f32[1,256]{1,0:T(1,128)} %get-tuple-element.18) | copy-start | bytes 3076
  102.0 4.6 %copy-start = (f32[1024,128]{1,0:T(8,128)S(1)}, f32[1024,128]{1,0:T(8,128)}, u32[]{:S(2)}) copy-start(f32[1024,128]{1,0:T(8,128)} %get-tuple-element.33) | copy-start | bytes 1572868
  102.0 5.4 %copy-start.4 = (f32[1,128]{1,0:T(1,128)S(1)}, f32[1,128]{1,0:T(1,128)}, u32[]{:S(2)}) copy-start(f32[1,128]{1,0:T(1,128)} %get-tuple-element.20) | copy-start | bytes 1540

commit v3 on v2

--- a/solution.py
+++ b/solution.py
@@ -119,11 +119,9 @@
     dwb,
     obacc,
     a1,
-    s1,
-    a2,
     a3,
-    a4,
     a5,
+    grads,
     pwt,
     vec,
     acc,
@@ -153,16 +151,12 @@
     sl1_recv,
     sl2_send,
     sl2_recv,
-    a_row_send,
-    a_row_recv,
-    a_col_send,
-    a_col_recv,
+    a_part_send,
+    a_part_recv,
     a_tgt_send,
     a_tgt_recv,
-    a_col2_send,
-    a_col2_recv,
-    a_row2_send,
-    a_row2_recv,
+    a_whole_send,
+    a_whole_recv,
     b_row_send,
     b_row_recv,
     b_col_send,
@@ -276,21 +270,27 @@
         at = left_block(cs(2), k)
         return at, at, gl2_send.at[k], gl2_recv.at[k], to_c(k)
 
-    def first_right(k):
-        to = rt.at[:, q_at, pl.ds(pl.multiple_of(c * rl, rl), rl), :]
-        return rown, to, gr1_send.at[k], gr1_recv.at[q_at], {"row": k * nx + c, "col": home}
-
-    def first_right_in(k):
-        to = rt.at[:, k, pl.ds(pl.multiple_of(x_at * rl, rl), rl), :]
-        return rown, to, gr1_send.at[k], gr1_recv.at[k], {"row": rpc * c + k, "col": x_at}
-
-    def gather_right(k):
-        at = right_block(x_at)
-        return at, at, gr_send.at[k], gr_recv.at[k], to_x(k)
-
-    def gather_right_in(k):
-        at = right_block(xs(back_of[k]))
-        return at, at, gr_send.at[k], gr_recv.at[k], to_x(k)
+    def first_right(k, part):
+        at = pl.ds(pl.multiple_of(c * rl, rl), rl)
+        rows = slice(part * half, (part + 1) * half)
+        to = rt.at[rows, q_at, at, :]
+        where = {"row": k * nx + c, "col": home}
+        return rown.at[rows], to, gr1_send.at[k, part], gr1_recv.at[q_at, part], where
+
+    def first_right_in(k, part):
+        at = pl.ds(pl.multiple_of(x_at * rl, rl), rl)
+        rows = slice(part * half, (part + 1) * half)
+        to = rt.at[rows, k, at, :]
+        where = {"row": rpc * c + k, "col": x_at}
+        return rown.at[rows], to, gr1_send.at[k, part], gr1_recv.at[k, part], where
+
+    def gather_right(k, part):
+        at = right_block(x_at, part)
+        return at, at, gr_send.at[k, part], gr_recv.at[k, part], to_x(k)
+
+    def gather_right_in(k, part):
+        at = right_block(xs(back_of[k]), part)
+        return at, at, gr_send.at[k, part], gr_recv.at[k, part], to_x(k)
 
     def relay_right(k):
         at = right_block(xs(back_of[k]), k)
@@ -303,8 +303,9 @@
     def unless(same, act):
         pl.when(jnp.logical_not(jnp.logical_and(own, same)))(act)
 
-    for k in range(rpc):
-        unless(z == k, lambda: push(*first_right(k)))
+    for part in range(2):
+        for k in range(rpc):
+            unless(z == k, lambda: push(*first_right(k, part)))
 
     @pl.when(own)
     def _():
@@ -326,24 +327,26 @@
         obacc[...] += jnp.sum(rows.astype(F32).reshape(2 * nj // 8, 8, CZ), 0)
         return 0
 
-    lax.fori_loop(0, ni // 4, back, 0)
+    lax.fori_loop(0, 6 * ni // 32, back, 0, unroll=2)
+    for k in range(2):
+        arrived(*gather_left_in(k))
+        push(*relay_left(k))
+    lax.fori_loop(6 * ni // 32, 9 * ni // 32, back, 0, unroll=2)
     for k in range(rpc):
-        unless(q_at == k, lambda: arrived(*first_right_in(k)))
-    for k in range(2):
-        push(*gather_right(k))
-    for k in range(2):
-        arrived(*gather_left_in(k))
-    for k in range(2):
-        push(*relay_left(k))
-    lax.fori_loop(ni // 4, ni // 2, back, 0)
-
-    for k in range(2):
-        arrived(*gather_right_in(k))
-    for k in range(2):
-        push(*relay_right(k))
+        unless(q_at == k, lambda: arrived(*first_right_in(k, 0)))
+    for k in range(2):
+        push(*gather_right(k, 0))
+    lax.fori_loop(9 * ni // 32, 11 * ni // 32, back, 0, unroll=2)
+    for k in range(rpc):
+        unless(q_at == k, lambda: arrived(*first_right_in(k, 1)))
+    for k in range(2):
+        push(*gather_right(1 - k, 1))
+    lax.fori_loop(11 * ni // 32, ni // 2, back, 0, unroll=2)
+    arrived(*gather_right_in(0, 0))
+    push(*relay_right(0))
+
     for k in range(2):
         arrived(*relay_left_in(k))
-
     def flip(k, _):
         at = pl.ds(pl.multiple_of(k * 128, 128), 128)
         lmat[:, at] = lt[at, :].T
@@ -352,12 +355,10 @@
     lax.fori_loop(0, ni * CH // 128, flip, 0)
 
     def right_step(k, _):
-        lanes = pl.ds(pl.multiple_of(k * 2 * nj, 2 * nj), 2 * nj)
+        lanes = pl.ds(pl.multiple_of(k * 8 * nj, 8 * nj), 8 * nj)
         y = mm(lmat[...], pair[:, lanes]).T
-        rp[pl.ds(2 * k, 2)] = y.reshape(2, rpc, nj // rpc, S).astype(BF16)
-        return 0
-
-    lax.fori_loop(0, CH // 2, right_step, 0)
+        rp[pl.ds(8 * k, 8)] = y.reshape(8, rpc, nj // rpc, S).astype(BF16)
+        return 0
 
     def right_sum(k, part=None):
         at = pl.ds(pl.multiple_of(k * rl, rl), rl)
@@ -368,9 +369,10 @@
     def far_right(k):
         return right_sum(xs(2), k), ra.at[k], sr1_send.at[k], sr1_recv.at[k], to_x(k)
 
-    def near_right(k):
-        at = right_sum(xs(1 if k == 0 else 3))
-        return at, rb.at[k], sr2_send.at[k], sr2_recv.at[k], to_x(k)
+    def near_right(k, part):
+        at = right_sum(xs(1 if k == 0 else 3), part)
+        to = rb.at[k, part * half : (part + 1) * half]
+        return at, to, sr2_send.at[k, part], sr2_recv.at[k, part], to_x(k)
 
     def scatter_right(k):
         where = {"row": rpc * c + k, "col": x_at}
@@ -380,9 +382,17 @@
         where = {"row": k * nx + c, "col": home}
         return ms.at[k], rr.at[k], sr3_send.at[k], sr3_recv.at[k], where
 
-    for k in range(2):
-        push(*far_right(k))
-
+    lax.fori_loop(0, CH // 16, right_step, 0)
+    push(*far_right(0))
+    push(*near_right(1, 0))
+    arrived(*gather_right_in(1, 1))
+    push(*relay_right(1))
+    lax.fori_loop(CH // 16, CH // 8, right_step, 0)
+    push(*far_right(1))
+    push(*near_right(0, 1))
+
+    for k in range(2):
+        arrived(*gather_right_in(k, 1 - k))
     for k in range(2):
         arrived(*relay_right_in(k))
 
@@ -408,10 +418,9 @@
     left_step(cs(1), 0)
     for k in range(2):
         arrived(*far_right(k))
-    for k in range(2):
         at = right_sum(xs(1 if k == 0 else 3), k)
         at[...] = (at[...].astype(F32) + ra[k].astype(F32)).astype(BF16)
-        push(*near_right(k))
+        push(*near_right(k, k))
     left_step(cs(3), 0)
     for k in range(2):
         arrived(*far_left(k))
@@ -436,9 +445,10 @@
         dw[...] += mm(on[...], g[pl.ds(pl.multiple_of(k * 8 * nj, 8 * nj), 8 * nj), :])
         return 0
 
-    lax.fori_loop(0, ni // 16, weigh, 0)
-    for k in range(2):
-        arrived(*near_right(k))
+    lax.fori_loop(0, ni // 32, weigh, 0)
+    for k in range(2):
+        for part in range(2):
+            arrived(*near_right(k, part))
     for k in range(rpc):
         at = pl.ds(pl.multiple_of(x_at * rl, rl), rl)
         total = rp[:, k, at, :].astype(F32)
@@ -452,25 +462,43 @@
     def _():
         rr[z] = ms[q_at]
 
-    lax.fori_loop(ni // 16, ni // 8, weigh, 0)
-
-    ar = CH * CH // nr
-    ac = ar // nc
-
-    def a_row(k):
-        q = lax.rem(r + k, nr)
-        src = dwb.at[pl.ds(pl.multiple_of(q * ar, ar), ar), :]
-        return src, a1.at[r], a_row_send.at[k], a_row_recv.at[r], {"row": q}
-
-    def a_row_in(k):
-        q = lax.rem(r + k, nr)
-        src = dwb.at[pl.ds(0, ar), :]
-        return src, a1.at[q], a_row_send.at[k], a_row_recv.at[q], {"row": q}
+    lax.fori_loop(ni // 32, ni // 8, weigh, 0)
+
+    group = nr * nc
+    flat = r * nc + c
+
+    def member(k):
+        f = lax.rem(flat + k, group)
+        return f, {"row": lax.div(f, nc), "col": lax.rem(f, nc)}
+
+    def a_part(k):
+        f, where = member(k)
+        src = dwb.at[pl.ds(pl.multiple_of(f * CH, CH), CH), :]
+        return src, a1.at[flat], a_part_send.at[k], a_part_recv.at[flat], where
+
+    def a_part_in(k):
+        f, where = member(k)
+        src = dwb.at[pl.ds(pl.multiple_of(flat * CH, CH), CH), :]
+        return src, a1.at[f], a_part_send.at[k], a_part_recv.at[f], where
+
+    def a_whole(k):
+        _, where = member(k)
+        return a5.at[flat], a5.at[flat], a_whole_send.at[k], a_whole_recv.at[flat], where
+
+    def a_whole_in(k):
+        f, where = member(k)
+        return a5.at[f], a5.at[f], a_whole_send.at[k], a_whole_recv.at[f], where
+
+    def every(act, copy):
+        def step(k, _):
+            act(*copy(k))
+            return 0
+
+        lax.fori_loop(1, group, step, 0)
 
     dwb[...] = dw[...].astype(BF16)
-    for k in range(1, nr):
-        push(*a_row(k))
-    a1[r] = dwb[pl.ds(pl.multiple_of(r * ar, ar), ar), :]
+    every(push, a_part)
+    a1[flat] = dwb[pl.ds(pl.multiple_of(flat * CH, CH), CH), :]
 
     for k in range(2):
         arrived(*near_left(k))
@@ -497,26 +525,6 @@
         return 0
 
     lax.fori_loop(0, CH // 8, sum_right, 0)
-
-    for k in range(1, nr):
-        arrived(*a_row_in(k))
-    total = a1[0].astype(F32)
-    for q in range(1, nr):
-        total += a1[q].astype(F32)
-    s1[...] = total
-
-    def a_col(k):
-        q = lax.rem(c + k, nc)
-        src = s1.at[pl.ds(pl.multiple_of(q * ac, ac), ac), :]
-        return src, a2.at[c], a_col_send.at[k], a_col_recv.at[c], {"col": q}
-
-    def a_col_in(k):
-        q = lax.rem(c + k, nc)
-        return s1.at[pl.ds(0, ac), :], a2.at[q], a_col_send.at[k], a_col_recv.at[q], {"col": q}
-
-    for k in range(1, nc):
-        push(*a_col(k))
-    a2[c] = s1[pl.ds(pl.multiple_of(c * ac, ac), ac), :]
 
     pwt[...] = jnp.zeros_like(pwt)
     acc[...] = jnp.zeros_like(acc)
@@ -529,16 +537,12 @@
         turned = both.T
         acc[:, 2 * CM : 2 * CM + 2 * CH] += jnp.sum(turned.reshape(S // 8, 8, 2 * CH), 0)
         grad = mm(turned.astype(BF16), pt)
+        grads[pl.ds(pl.multiple_of(k * S, S), S), :] = grad
         pwt[...] += mm(rounded, no[pl.ds(pl.multiple_of(k * S, S), S), :])
         at = pl.ds(k, S, stride=rl)
         x = jnp.concatenate([nrm[0, at, :], nrm[1, at, :]], 1)
-        scale = inv[at, :]
         acc[:, :CM] += jnp.sum((grad * x).reshape(S // 8, 8, CM), 0)
         acc[:, CM : 2 * CM] += jnp.sum(grad.reshape(S // 8, 8, CM), 0)
-        scaled = grad * mult
-        dx = scaled - jnp.mean(scaled, -1, keepdims=True) - x * jnp.mean(scaled * x, -1, keepdims=True)
-        nrm[0, at, :] = dx[:, :128] * scale
-        nrm[1, at, :] = dx[:, 128:] * scale
         return 0
 
     lax.fori_loop(0, rl, finish, 0)
@@ -570,11 +574,10 @@
         push(*b_row(k))
     b1[r] = sb[r]
 
-    for k in range(1, nc):
-        arrived(*a_col_in(k))
-    total = a2[0]
-    for q in range(1, nc):
-        total += a2[q]
+    every(arrived, a_part_in)
+    total = a1[0].astype(F32)
+    for q in range(1, group):
+        total += a1[q].astype(F32)
     a3[t] = total
 
     def a_tgt(k):
@@ -588,15 +591,18 @@
     for k in range(1, nt):
         push(*a_tgt(k))
 
-    def emit(k, _):
-        rows = pl.ds(pl.multiple_of(k * 128, 128), 128)
-        h[rows, :128] = nrm[0, rows, :].astype(BF16)
-        h[rows, 128:] = nrm[1, rows, :].astype(BF16)
-        return 0
-
-    lax.fori_loop(0, S * rl // 128, emit, 0)
-    dx_copy = pltpu.make_async_copy(h, dx_out, local_sem.at[2])
-    dx_copy.start()
+    def descend(k, _):
+        grad = grads[pl.ds(pl.multiple_of(k * S, S), S), :]
+        at = pl.ds(k, S, stride=rl)
+        x = jnp.concatenate([nrm[0, at, :], nrm[1, at, :]], 1)
+        scale = inv[at, :]
+        scaled = grad * mult
+        dx = scaled - jnp.mean(scaled, -1, keepdims=True) - x * jnp.mean(scaled * x, -1, keepdims=True)
+        nrm[0, at, :] = dx[:, :128] * scale
+        nrm[1, at, :] = dx[:, 128:] * scale
+        return 0
+
+    lax.fori_loop(0, rl // 2, descend, 0)
 
     for k in range(1, nr):
         arrived(*b_row_in(k))
@@ -616,23 +622,17 @@
     for k in range(1, nc):
         push(*b_col(k))
 
-    for k in range(1, nt):
-        arrived(*a_tgt_in(k))
-    total = a3[0]
-    for q in range(1, nt):
-        total += a3[q]
-    a4[c] = total.astype(BF16)
-
-    def a_col2(k):
-        q = lax.rem(c + k, nc)
-        return a4.at[c], a4.at[c], a_col2_send.at[k], a_col2_recv.at[c], {"col": q}
-
-    def a_col2_in(k):
-        q = lax.rem(c + k, nc)
-        return a4.at[q], a4.at[q], a_col2_send.at[k], a_col2_recv.at[q], {"col": q}
-
-    for k in range(1, nc):
-        push(*a_col2(k))
+    lax.fori_loop(rl // 2, rl, descend, 0)
+
+    def emit(k, _):
+        rows = pl.ds(pl.multiple_of(k * 128, 128), 128)
+        h[rows, :128] = nrm[0, rows, :].astype(BF16)
+        h[rows, 128:] = nrm[1, rows, :].astype(BF16)
+        return 0
+
+    lax.fori_loop(0, S * rl // 128, emit, 0)
+    dx_copy = pltpu.make_async_copy(h, dx_out, local_sem.at[2])
+    dx_copy.start()
 
     for k in range(1, nc):
         arrived(*b_col_in(k))
@@ -652,20 +652,13 @@
     for k in range(1, nt):
         push(*b_tgt(k))
 
-    for k in range(1, nc):
-        arrived(*a_col2_in(k))
-    a5[r] = a4[...].reshape(ar, CZ)
-
-    def a_row2(k):
-        q = lax.rem(r + k, nr)
-        return a5.at[r], a5.at[r], a_row2_send.at[k], a_row2_recv.at[r], {"row": q}
-
-    def a_row2_in(k):
-        q = lax.rem(r + k, nr)
-        return a5.at[q], a5.at[q], a_row2_send.at[k], a_row2_recv.at[q], {"row": q}
-
-    for k in range(1, nr):
-        push(*a_row2(k))
+    for k in range(1, nt):
+        arrived(*a_tgt_in(k))
+    total = a3[0]
+    for q in range(1, nt):
+        total += a3[q]
+    a5[flat] = total.astype(BF16)
+    every(push, a_whole)
 
     for k in range(1, nt):
         arrived(*b_tgt_in(k))
@@ -686,13 +679,10 @@
         push(*b_row2(k))
 
     factor = 1.0 / (nt * nr * nc * rl)
-    for k in range(1, nr):
-        arrived(*a_row2_in(k))
+    every(arrived, a_whole_in)
 
     def place(d, _):
-        at = pl.multiple_of(d * CH, CH)
-        rows = a5[lax.div(at, ar), pl.ds(pl.multiple_of(lax.rem(at, ar), CH), CH), :]
-        ow_out[pl.ds(d, CH, stride=CH), :] = rows.astype(F32) * (factor / S)
+        ow_out[pl.ds(d, CH, stride=CH), :] = a5[d].astype(F32) * (factor / S)
         return 0
 
     lax.fori_loop(0, CH, place, 0)
@@ -713,22 +703,20 @@
     for k in range(2):
         sent(*gather_left(k))
         sent(*relay_left(k))
-        sent(*gather_right(k))
         sent(*relay_right(k))
         sent(*far_right(k))
-        sent(*near_right(k))
         sent(*far_left(k))
         sent(*near_left(k))
-    for k in range(rpc):
-        unless(z == k, lambda: sent(*first_right(k)))
+        for part in range(2):
+            sent(*gather_right(k, part))
+            sent(*near_right(k, part))
+            unless(z == k, lambda: sent(*first_right(k, part)))
         unless(q_at == k, lambda: sent(*scatter_right(k)))
+    every(sent, a_part)
+    every(sent, a_whole)
     for k in range(1, nc):
-        sent(*a_col(k))
-        sent(*a_col2(k))
         sent(*b_col(k))
     for k in range(1, nr):
-        sent(*a_row(k))
-        sent(*a_row2(k))
         sent(*b_row(k))
         sent(*b_row2(k))
     for k in range(1, nt):
@@ -748,13 +736,12 @@
     nt, nr, nc = axis_sizes()
     rl = homolog_activation_matrix.shape[2]
     ni, nj = rl * nc, rl * nr
-    ar = CH * CH // nr
     pr = 4 * CH // nr + 8
     vmem = functools.partial(pl.BlockSpec, memory_space=pltpu.VMEM)
     hbm = functools.partial(pl.BlockSpec, memory_space=pl.ANY)
 
-    def sems(n):
-        return [pltpu.SemaphoreType.DMA((n,)), pltpu.SemaphoreType.DMA((n,))]
+    def sems(*n):
+        return [pltpu.SemaphoreType.DMA(n), pltpu.SemaphoreType.DMA(n)]
 
     results = pl.pallas_call(
         functools.partial(kernel, (nt, nr, nc, rl)),
@@ -796,12 +783,10 @@
             pltpu.VMEM((CH * CH, CZ), F32),
             pltpu.VMEM((CH * CH, CZ), BF16),
             pltpu.VMEM((8, CZ), F32),
-            pltpu.VMEM((nr, ar, CZ), BF16),
-            pltpu.VMEM((ar, CZ), F32),
-            pltpu.VMEM((nc, ar // nc, CZ), F32),
-            pltpu.VMEM((nt, ar // nc, CZ), F32),
-            pltpu.VMEM((nc, ar // nc, CZ), BF16),
-            pltpu.VMEM((nr, ar, CZ), BF16),
+            pltpu.VMEM((nr * nc, CH, CZ), BF16),
+            pltpu.VMEM((nt, CH, CZ), F32),
+            pltpu.VMEM((nr * nc, CH, CZ), BF16),
+            pltpu.VMEM((S * rl, CM), F32),
             pltpu.VMEM((2 * CH, CM), F32),
             pltpu.VMEM((8, 128), F32),
             pltpu.VMEM((8, 2 * CM + 128), F32),
@@ -812,12 +797,16 @@
             pltpu.VMEM((nr, pr, 128), F32),
             pltpu.SemaphoreType.DMA((3,)),
         ]
-        + 10 * sems(2)
-        + sems(nr)
-        + sems(nc)
+        + sems(2)
+        + sems(2)
+        + 2 * sems(2, 2)
+        + sems(2)
+        + sems(2)
+        + sems(2, 2)
+        + 3 * sems(2)
+        + sems(nr * nc)
         + sems(nt)
-        + sems(nc)
-        + sems(nr)
+        + sems(nr * nc)
         + sems(nr)
         + sems(nc)
         + sems(nt)

time: 108 us -> 106 us (0.981)
  Pallas kernels: 101 us -> 99.4 us
    pallas_call x1, Pallas kernels: 101 us -> 99.4 us  [per_device(): pl.pallas_call(functools.partial(kernel, (nt, nr, nc, rl)), out_shape=(ja...]
where the time goes in v3:
time: 106 us
  Pallas kernels  99.4 us (94%)
  local copies, waits for them, and re-layouts  5.92 us (6%)
    pallas_call x1, Pallas kernels, per_device(): pl.pallas_call(functools.partial(kernel, (nt, nr, nc, rl)), out_shape=(ja...  99.4 us
    unnamed x19, local copies, waits for them, and re-layouts  5.92 us

profile of v3, /device:TPU:1, one launch (start us, length us, event | category | flops | bytes accessed | tf_op | source)
XLA Modules:
  0.0 106.0 jit_solution(1121278197389886593)
XLA Ops:
  0.6 99.4 %shard_map.126 = (bf16[2048,256]{1,0:T(8,128)(2,1)}, f32[64,256]{1,0:T(8,128)}, f32[1,64]{1,0:T(1,128)}, f32[1,256]{1,0:T(1,128)}, f32[1,256]{1,0:T(1,128)}, /*index=5*/f32[1024,128]{1,0:T(8,128)}, f32[1,128]{1,0:T(1,128)}) custom-call(bf16[2048,256]{1,0:T(8,128)(2,1)} %bitcast.17, f32[1,256]{1,0:T(1,128)} %bitcast.19, f32[1,256]{1,0:T(1,128)} %bitcast.20, ...), custom_call_target="tpu_custom_call" | custom-call | flops 10737418240 | bytes 5242880 | tf_op jit(solution)/shard_map/pallas_call | solution.py:746
  100.1 0.0 copy-start.1
  100.1 0.0 copy-start.5
  100.1 0.0 copy-start.3
  100.1 0.0 copy-start.2
  100.1 0.0 copy-start
  100.1 0.0 copy-start.4
  100.1 2.3 %copy.21 = bf16[1,128,16,256]{3,2,1,0:T(8,128)(2,1)} copy(bf16[1,128,16,256]{3,2,1,0:T(8,128)(2,1)} %bitcast.12) | data formatting | bytes 2097152
  102.5 0.0 copy-done.1
  102.5 0.6 copy.22
  103.1 0.0 copy-done.5
  103.1 0.5 copy.23
  103.6 0.0 copy-done.3
  103.6 0.6 copy.24
  104.2 0.0 copy-done.2
  104.2 0.6 copy.25
  104.7 0.0 copy-done
  104.7 0.8 copy.26
  105.5 0.0 copy-done.4
  105.5 0.5 copy.27
Async XLA Ops:
  100.1 2.4 %copy-start.1 = (f32[64,256]{1,0:T(8,128)S(1)}, f32[64,256]{1,0:T(8,128)}, u32[]{:S(2)}) copy-start(f32[64,256]{1,0:T(8,128)} %get-tuple-element.15) | copy-start | bytes 196612
  100.1 3.0 %copy-start.5 = (f32[1,64]{1,0:T(1,128)S(1)}, f32[1,64]{1,0:T(1,128)}, u32[]{:S(2)}) copy-start(f32[1,64]{1,0:T(1,128)} %get-tuple-element.16) | copy-start | bytes 772
  100.1 3.5 %copy-start.3 = (f32[1,256]{1,0:T(1,128)S(1)}, f32[1,256]{1,0:T(1,128)}, u32[]{:S(2)}) copy-start(f32[1,256]{1,0:T(1,128)} %get-tuple-element.17) | copy-start | bytes 3076
  100.1 4.1 %copy-start.2 = (f32[1,256]{1,0:T(1,128)S(1)}, f32[1,256]{1,0:T(1,128)}, u32[]{:S(2)}) copy-start(f32[1,256]{1,0:T(1,128)} %get-tuple-element.18) | copy-start | bytes 3076
  100.1 4.6 %copy-start = (f32[1024,128]{1,0:T(8,128)S(1)}, f32[1024,128]{1,0:T(8,128)}, u32[]{:S(2)}) copy-start(f32[1024,128]{1,0:T(8,128)} %get-tuple-element.33) | copy-start | bytes 1572868
  100.1 5.4 %copy-start.4 = (f32[1,128]{1,0:T(1,128)S(1)}, f32[1,128]{1,0:T(1,128)}, u32[]{:S(2)}) copy-start(f32[1,128]{1,0:T(1,128)} %get-tuple-element.20) | copy-start | bytes 1540

commit v4 on v3

--- a/solution.py
+++ b/solution.py
@@ -175,7 +175,10 @@
     t, r, c = axis_places()
     home = lax.div(r, rpc)
     z, x_at, q_at = lax.div(r, nx), lax.rem(r, nx), lax.rem(r, rpc)
-    own = jnp.logical_and(x_at == c, home == c)
+    c_half, c_odd = lax.div(c, 2), lax.rem(c, 2)
+    side_x = lax.rem(x_at + jnp.where(lax.rem(x_at, 2) == 1, 1, nx - 1), nx)
+    via = jnp.where(c_odd == 1, side_x, x_at)
+    own = jnp.logical_and(via == x_at, home == c)
     half, lhalf = CH // 2, lrows // 2
 
     h_in = pltpu.make_async_copy(h_ref, h, local_sem.at[0])
@@ -249,11 +252,15 @@
         at, size = (k * lrows, lrows) if part is None else (k * lrows + part * lhalf, lhalf)
         return lt.at[pl.ds(pl.multiple_of(at, lhalf), size), :]
 
-    def right_block(k, part=None):
-        at = pl.ds(pl.multiple_of(k * rl, rl), rl)
-        if part is None:
-            return rt.at[:, :, at, :]
-        return rt.at[part * half : (part + 1) * half, :, at, :]
+    def spot(x):
+        e = lax.rem(x + nx - 2 * c_odd, nx)
+        return lax.div(lax.rem(e + 1, nx), 2), lax.div(e, 2)
+
+    my_q, my_odd = spot(x_at)
+
+    def right_block(x, part):
+        q, odd = spot(x)
+        return rt.at[part * half : (part + 1) * half, q, :, odd]
 
     def gather_left(k):
         return left_block(c), left_block(c), gl_send.at[k], gl_recv.at[k], to_c(k)
@@ -271,17 +278,15 @@
         return at, at, gl2_send.at[k], gl2_recv.at[k], to_c(k)
 
     def first_right(k, part):
-        at = pl.ds(pl.multiple_of(c * rl, rl), rl)
         rows = slice(part * half, (part + 1) * half)
-        to = rt.at[rows, q_at, at, :]
-        where = {"row": k * nx + c, "col": home}
-        return rown.at[rows], to, gr1_send.at[k, part], gr1_recv.at[q_at, part], where
+        to = rt.at[rows, q_at, c_half, c_odd]
+        where = {"row": k * nx + via, "col": home}
+        return rown.at[rows], to, gr1_send.at[k, part], gr1_recv.at[c_half, part], where
 
     def first_right_in(k, part):
-        at = pl.ds(pl.multiple_of(x_at * rl, rl), rl)
         rows = slice(part * half, (part + 1) * half)
-        to = rt.at[rows, k, at, :]
-        where = {"row": rpc * c + k, "col": x_at}
+        to = rt.at[rows, my_q, k, my_odd]
+        where = {"row": rpc * c + my_q, "col": 2 * k + my_odd}
         return rown.at[rows], to, gr1_send.at[k, part], gr1_recv.at[k, part], where
 
     def gather_right(k, part):
@@ -309,7 +314,7 @@
 
     @pl.when(own)
     def _():
-        rt[:, q_at, pl.ds(pl.multiple_of(c * rl, rl), rl), :] = rown[...]
+        rt[:, q_at, c_half, c_odd] = rown[...]
 
     for k in range(2):
         push(*gather_left(k))
@@ -333,12 +338,12 @@
         push(*relay_left(k))
     lax.fori_loop(6 * ni // 32, 9 * ni // 32, back, 0, unroll=2)
     for k in range(rpc):
-        unless(q_at == k, lambda: arrived(*first_right_in(k, 0)))
+        unless(c_half == k, lambda: arrived(*first_right_in(k, 0)))
     for k in range(2):
         push(*gather_right(k, 0))
     lax.fori_loop(9 * ni // 32, 11 * ni // 32, back, 0, unroll=2)
     for k in range(rpc):
-        unless(q_at == k, lambda: arrived(*first_right_in(k, 1)))
+        unless(c_half == k, lambda: arrived(*first_right_in(k, 1)))
     for k in range(2):
         push(*gather_right(1 - k, 1))
     lax.fori_loop(11 * ni // 32, ni // 2, back, 0, unroll=2)
@@ -357,14 +362,12 @@
     def right_step(k, _):
         lanes = pl.ds(pl.multiple_of(k * 8 * nj, 8 * nj), 8 * nj)
         y = mm(lmat[...], pair[:, lanes]).T
-        rp[pl.ds(8 * k, 8)] = y.reshape(8, rpc, nj // rpc, S).astype(BF16)
-        return 0
-
-    def right_sum(k, part=None):
-        at = pl.ds(pl.multiple_of(k * rl, rl), rl)
-        if part is None:
-            return rp.at[:, :, at, :]
-        return rp.at[part * half : (part + 1) * half, :, at, :]
+        rp[pl.ds(8 * k, 8)] = y.reshape(8, 2, 2, 2, rl, S).astype(BF16)
+        return 0
+
+    def right_sum(x, part):
+        q, odd = spot(x)
+        return rp.at[part * half : (part + 1) * half, q, :, odd]
 
     def far_right(k):
         return right_sum(xs(2), k), ra.at[k], sr1_send.at[k], sr1_recv.at[k], to_x(k)
@@ -375,11 +378,11 @@
         return at, to, sr2_send.at[k, part], sr2_recv.at[k, part], to_x(k)
 
     def scatter_right(k):
-        where = {"row": rpc * c + k, "col": x_at}
+        where = {"row": rpc * c + my_q, "col": 2 * k + my_odd}
         return ms.at[k], rr.at[z], sr3_send.at[k], sr3_recv.at[z], where
 
     def scatter_right_in(k):
-        where = {"row": k * nx + c, "col": home}
+        where = {"row": k * nx + via, "col": home}
         return ms.at[k], rr.at[k], sr3_send.at[k], sr3_recv.at[k], where
 
     lax.fori_loop(0, CH // 16, right_step, 0)
@@ -450,17 +453,16 @@
         for part in range(2):
             arrived(*near_right(k, part))
     for k in range(rpc):
-        at = pl.ds(pl.multiple_of(x_at * rl, rl), rl)
-        total = rp[:, k, at, :].astype(F32)
+        total = rp[:, my_q, k, my_odd].astype(F32)
         total += rb[0, :, k].astype(F32)
         total += rb[1, :, k].astype(F32)
         ms[k] = total.astype(BF16)
     for k in range(rpc):
-        unless(q_at == k, lambda: push(*scatter_right(k)))
+        unless(c_half == k, lambda: push(*scatter_right(k)))
 
     @pl.when(own)
     def _():
-        rr[z] = ms[q_at]
+        rr[z] = ms[c_half]
 
     lax.fori_loop(ni // 32, ni // 8, weigh, 0)
 
@@ -687,6 +689,27 @@
 
     lax.fori_loop(0, CH, place, 0)
 
+    for k in range(2):
+        sent(*gather_left(k))
+        sent(*relay_left(k))
+        sent(*relay_right(k))
+        sent(*far_right(k))
+        sent(*far_left(k))
+        sent(*near_left(k))
+        for part in range(2):
+            sent(*gather_right(k, part))
+            sent(*near_right(k, part))
+            unless(z == k, lambda: sent(*first_right(k, part)))
+        unless(c_half == k, lambda: sent(*scatter_right(k)))
+    every(sent, a_part)
+    for k in range(1, nc):
+        sent(*b_col(k))
+    for k in range(1, nr):
+        sent(*b_row(k))
+    for k in range(1, nt):
+        sent(*a_tgt(k))
+        sent(*b_tgt(k))
+    dx_copy.wait()
     for k in range(1, nr):
         arrived(*b_row2_in(k))
     whole = b4[:, :pr, :].reshape(4 * CH, 128) * factor
@@ -699,29 +722,9 @@
     shift_out[...] = jnp.concatenate([vec[3:4, :], vec[4:5, :]], 1)
     ob_out[...] = vec[5:6, :]
 
-    dx_copy.wait()
-    for k in range(2):
-        sent(*gather_left(k))
-        sent(*relay_left(k))
-        sent(*relay_right(k))
-        sent(*far_right(k))
-        sent(*far_left(k))
-        sent(*near_left(k))
-        for part in range(2):
-            sent(*gather_right(k, part))
-            sent(*near_right(k, part))
-            unless(z == k, lambda: sent(*first_right(k, part)))
-        unless(q_at == k, lambda: sent(*scatter_right(k)))
-    every(sent, a_part)
     every(sent, a_whole)
-    for k in range(1, nc):
-        sent(*b_col(k))
     for k in range(1, nr):
-        sent(*b_row(k))
         sent(*b_row2(k))
-    for k in range(1, nt):
-        sent(*a_tgt(k))
-        sent(*b_tgt(k))
 
 
 def per_device(
@@ -764,13 +767,13 @@
             pltpu.VMEM((S * rl, CM), BF16),
             pltpu.VMEM((ni * CH, S), BF16),
             pltpu.VMEM((S, ni * CH), BF16),
-            pltpu.VMEM((CH, 2, nj // 2, S), BF16),
+            pltpu.VMEM((CH, 2, 2, 2, rl, S), BF16),
             pltpu.VMEM((CH, rl, S), BF16),
             pltpu.VMEM((rl * CH, S), F32),
             pltpu.VMEM((CH * CH, CZ), F32),
             pltpu.VMEM((CH * CH, CZ), BF16),
             pltpu.VMEM((ni * CH, CH * nj), BF16),
-            pltpu.VMEM((CH, 2, nj // 2, S), BF16),
+            pltpu.VMEM((CH, 2, 2, 2, rl, S), BF16),
             pltpu.VMEM((nc, rl * CH, S), BF16),
             pltpu.VMEM((2, CH // 2, 2, rl, S), BF16),
             pltpu.VMEM((2, CH, 2, rl, S), BF16),

time: 106 us -> 97.4 us (0.919)
  Pallas kernels: 99.4 us -> 90.6 us
    pallas_call x1, Pallas kernels: 99.4 us -> 90.6 us  [per_device(): pl.pallas_call(functools.partial(kernel, (nt, nr, nc, rl)), out_shape=(ja...]
where the time goes in v4:
time: 97.4 us; the launch traced here: 97.3 us
  Pallas kernels  90.6 us (93%)
  local copies, waits for them, and re-layouts  5.92 us (6%)
    pallas_call x1, Pallas kernels, per_device(): pl.pallas_call(functools.partial(kernel, (nt, nr, nc, rl)), out_shape=(ja...  90.6 us
    unnamed x19, local copies, waits for them, and re-layouts  5.92 us

profile of v4, /device:TPU:1, one launch (start us, length us, event | category | flops | bytes accessed | tf_op | source)
XLA Modules:
  0.0 97.3 jit_solution(14478024906951805912)
XLA Ops:
  0.6 90.6 %shard_map.126 = (bf16[2048,256]{1,0:T(8,128)(2,1)}, f32[64,256]{1,0:T(8,128)}, f32[1,64]{1,0:T(1,128)}, f32[1,256]{1,0:T(1,128)}, f32[1,256]{1,0:T(1,128)}, /*index=5*/f32[1024,128]{1,0:T(8,128)}, f32[1,128]{1,0:T(1,128)}) custom-call(bf16[2048,256]{1,0:T(8,128)(2,1)} %bitcast.17, f32[1,256]{1,0:T(1,128)} %bitcast.19, f32[1,256]{1,0:T(1,128)} %bitcast.20, ...), custom_call_target="tpu_custom_call" | custom-call | flops 10737418240 | bytes 5242880 | tf_op jit(solution)/shard_map/pallas_call | solution.py:749
  91.3 0.0 copy-start.1
  91.3 0.0 copy-start.5
  91.3 0.0 copy-start.3
  91.3 0.0 copy-start.2
  91.3 0.0 copy-start
  91.3 0.0 copy-start.4
  91.3 2.3 %copy.21 = bf16[1,128,16,256]{3,2,1,0:T(8,128)(2,1)} copy(bf16[1,128,16,256]{3,2,1,0:T(8,128)(2,1)} %bitcast.12) | data formatting | bytes 2097152
  93.7 0.0 copy-done.1
  93.7 0.6 copy.22
  94.3 0.0 copy-done.5
  94.3 0.5 copy.23
  94.8 0.0 copy-done.3
  94.8 0.6 copy.24
  95.4 0.0 copy-done.2
  95.4 0.6 copy.25
  95.9 0.0 copy-done
  95.9 0.8 copy.26
  96.7 0.0 copy-done.4
  96.7 0.5 copy.27
Async XLA Ops:
  91.3 2.4 %copy-start.1 = (f32[64,256]{1,0:T(8,128)S(1)}, f32[64,256]{1,0:T(8,128)}, u32[]{:S(2)}) copy-start(f32[64,256]{1,0:T(8,128)} %get-tuple-element.15) | copy-start | bytes 196612
  91.3 3.0 %copy-start.5 = (f32[1,64]{1,0:T(1,128)S(1)}, f32[1,64]{1,0:T(1,128)}, u32[]{:S(2)}) copy-start(f32[1,64]{1,0:T(1,128)} %get-tuple-element.16) | copy-start | bytes 772
  91.3 3.5 %copy-start.3 = (f32[1,256]{1,0:T(1,128)S(1)}, f32[1,256]{1,0:T(1,128)}, u32[]{:S(2)}) copy-start(f32[1,256]{1,0:T(1,128)} %get-tuple-element.17) | copy-start | bytes 3076
  91.3 4.1 %copy-start.2 = (f32[1,256]{1,0:T(1,128)S(1)}, f32[1,256]{1,0:T(1,128)}, u32[]{:S(2)}) copy-start(f32[1,256]{1,0:T(1,128)} %get-tuple-element.18) | copy-start | bytes 3076
  91.3 4.6 %copy-start = (f32[1024,128]{1,0:T(8,128)S(1)}, f32[1024,128]{1,0:T(8,128)}, u32[]{:S(2)}) copy-start(f32[1024,128]{1,0:T(8,128)} %get-tuple-element.33) | copy-start | bytes 1572868
  91.3 5.4 %copy-start.4 = (f32[1,128]{1,0:T(1,128)S(1)}, f32[1,128]{1,0:T(1,128)}, u32[]{:S(2)}) copy-start(f32[1,128]{1,0:T(1,128)} %get-tuple-element.20) | copy-start | bytes 1540

commit v5 on v4

--- a/solution.py
+++ b/solution.py
@@ -106,6 +106,7 @@
     wp,
     pair,
     rp,
+    lsum,
     lp,
     ra,
     rb,
@@ -199,7 +200,7 @@
         wp[pl.ds(pl.multiple_of(d * CH, CH), CH), :] = rows.astype(BF16)
         return 0
 
-    lax.fori_loop(0, CH, reorder, 0)
+    lax.fori_loop(0, CH, reorder, 0, unroll=4)
     h_in.wait()
 
     def normalise(k, _):
@@ -213,7 +214,7 @@
         inv[rows, :] = jnp.broadcast_to(scale, (128, 128))
         return 0
 
-    lax.fori_loop(0, S * rl // 128, normalise, 0)
+    lax.fori_loop(0, S * rl // 128, normalise, 0, unroll=4)
 
     def project(k, _):
         at = pl.ds(k, S, stride=rl)
@@ -225,13 +226,13 @@
         rf[pl.ds(pl.multiple_of(k * CH, CH), CH), :] = y[CH:].astype(F32)
         return 0
 
-    lax.fori_loop(0, rl, project, 0)
+    lax.fori_loop(0, rl, project, 0, unroll=4)
 
     def turn(d, _):
         rown[d] = rf[pl.ds(d, rl, stride=CH), :].astype(BF16)
         return 0
 
-    lax.fori_loop(0, CH, turn, 0)
+    lax.fori_loop(0, CH, turn, 0, unroll=4)
     meet(nt, nr, nc)
 
     def xs(k):
@@ -357,7 +358,7 @@
         lmat[:, at] = lt[at, :].T
         return 0
 
-    lax.fori_loop(0, ni * CH // 128, flip, 0)
+    lax.fori_loop(0, ni * CH // 128, flip, 0, unroll=4)
 
     def right_step(k, _):
         lanes = pl.ds(pl.multiple_of(k * 8 * nj, 8 * nj), 8 * nj)
@@ -394,10 +395,8 @@
     push(*far_right(1))
     push(*near_right(0, 1))
 
-    for k in range(2):
-        arrived(*gather_right_in(k, 1 - k))
-    for k in range(2):
-        arrived(*relay_right_in(k))
+    arrived(*gather_right_in(1, 0))
+    arrived(*relay_right_in(0))
 
     def left_rows(k):
         return pl.ds(pl.multiple_of(k * lrows, lrows), lrows)
@@ -410,20 +409,28 @@
         at = lp.at[cs(1 if k == 0 else 3)]
         return at, lb.at[k], sl2_send.at[k], sl2_recv.at[k], to_c(k)
 
-    def left_step(k, _):
-        right_all = rt[...].reshape(CH * nj, S)
-        lp[k] = mm(pair[left_rows(k), :], right_all).astype(BF16)
-        return 0
-
-    left_step(cs(2), 0)
-    for k in range(2):
-        push(*far_left(k))
-    left_step(cs(1), 0)
+    def left_first(k, _):
+        lsum[k] = mm(pair[left_rows(k), : half * nj], rt[:half].reshape(half * nj, S))
+        return 0
+
+    lax.fori_loop(0, nc, left_first, 0)
     for k in range(2):
         arrived(*far_right(k))
         at = right_sum(xs(1 if k == 0 else 3), k)
         at[...] = (at[...].astype(F32) + ra[k].astype(F32)).astype(BF16)
         push(*near_right(k, k))
+    arrived(*gather_right_in(0, 1))
+    arrived(*relay_right_in(1))
+
+    def left_step(k, _):
+        more = mm(pair[left_rows(k), half * nj :], rt[half:].reshape(half * nj, S))
+        lp[k] = (lsum[k] + more).astype(BF16)
+        return 0
+
+    left_step(cs(2), 0)
+    for k in range(2):
+        push(*far_left(k))
+    left_step(cs(1), 0)
     left_step(cs(3), 0)
     for k in range(2):
         arrived(*far_left(k))
@@ -515,7 +522,7 @@
         side[at, :] = total * (1.0 / S)
         return 0
 
-    lax.fori_loop(0, lrows // 128, sum_left, 0)
+    lax.fori_loop(0, lrows // 128, sum_left, 0, unroll=4)
 
     def sum_right(k, _):
         at = pl.ds(k * 8, 8)
@@ -526,7 +533,7 @@
         side[to, :] = total.reshape(8 * rl, S) * (1.0 / S)
         return 0
 
-    lax.fori_loop(0, CH // 8, sum_right, 0)
+    lax.fori_loop(0, CH // 8, sum_right, 0, unroll=4)
 
     pwt[...] = jnp.zeros_like(pwt)
     acc[...] = jnp.zeros_like(acc)
@@ -547,7 +554,7 @@
         acc[:, CM : 2 * CM] += jnp.sum(grad.reshape(S // 8, 8, CM), 0)
         return 0
 
-    lax.fori_loop(0, rl, finish, 0)
+    lax.fori_loop(0, rl, finish, 0, unroll=4)
 
     pr = 2 * 2 * CH // nr
     vr = 8 // nr
@@ -604,7 +611,7 @@
         nrm[1, at, :] = dx[:, 128:] * scale
         return 0
 
-    lax.fori_loop(0, rl // 2, descend, 0)
+    lax.fori_loop(0, rl // 2, descend, 0, unroll=4)
 
     for k in range(1, nr):
         arrived(*b_row_in(k))
@@ -624,7 +631,7 @@
     for k in range(1, nc):
         push(*b_col(k))
 
-    lax.fori_loop(rl // 2, rl, descend, 0)
+    lax.fori_loop(rl // 2, rl, descend, 0, unroll=4)
 
     def emit(k, _):
         rows = pl.ds(pl.multiple_of(k * 128, 128), 128)
@@ -632,27 +639,9 @@
         h[rows, 128:] = nrm[1, rows, :].astype(BF16)
         return 0
 
-    lax.fori_loop(0, S * rl // 128, emit, 0)
+    lax.fori_loop(0, S * rl // 128, emit, 0, unroll=4)
     dx_copy = pltpu.make_async_copy(h, dx_out, local_sem.at[2])
     dx_copy.start()
-
-    for k in range(1, nc):
-        arrived(*b_col_in(k))
-    total = b2[0]
-    for q in range(1, nc):
-        total += b2[q]
-    b3[t] = total
-
-    def b_tgt(k):
-        q = lax.rem(t + k, nt)
-        return b3.at[t], b3.at[t], b_tgt_send.at[k], b_tgt_recv.at[t], {"tgt": q}
-
-    def b_tgt_in(k):
-        q = lax.rem(t + k, nt)
-        return b3.at[q], b3.at[q], b_tgt_send.at[k], b_tgt_recv.at[q], {"tgt": q}
-
-    for k in range(1, nt):
-        push(*b_tgt(k))
 
     for k in range(1, nt):
         arrived(*a_tgt_in(k))
@@ -662,6 +651,24 @@
     a5[flat] = total.astype(BF16)
     every(push, a_whole)
 
+    for k in range(1, nc):
+        arrived(*b_col_in(k))
+    total = b2[0]
+    for q in range(1, nc):
+        total += b2[q]
+    b3[t] = total
+
+    def b_tgt(k):
+        q = lax.rem(t + k, nt)
+        return b3.at[t], b3.at[t], b_tgt_send.at[k], b_tgt_recv.at[t], {"tgt": q}
+
+    def b_tgt_in(k):
+        q = lax.rem(t + k, nt)
+        return b3.at[q], b3.at[q], b_tgt_send.at[k], b_tgt_recv.at[q], {"tgt": q}
+
+    for k in range(1, nt):
+        push(*b_tgt(k))
+
     for k in range(1, nt):
         arrived(*b_tgt_in(k))
     total = b3[0]
@@ -687,7 +694,7 @@
         ow_out[pl.ds(d, CH, stride=CH), :] = a5[d].astype(F32) * (factor / S)
         return 0
 
-    lax.fori_loop(0, CH, place, 0)
+    lax.fori_loop(0, CH, place, 0, unroll=4)
 
     for k in range(2):
         sent(*gather_left(k))
@@ -774,6 +781,7 @@
             pltpu.VMEM((CH * CH, CZ), BF16),
             pltpu.VMEM((ni * CH, CH * nj), BF16),
             pltpu.VMEM((CH, 2, 2, 2, rl, S), BF16),
+            pltpu.VMEM((nc, rl * CH, S), F32),
             pltpu.VMEM((nc, rl * CH, S), BF16),
             pltpu.VMEM((2, CH // 2, 2, rl, S), BF16),
             pltpu.VMEM((2, CH, 2, rl, S), BF16),

time: 97.4 us -> 90.1 us (0.925)
  Pallas kernels: 90.6 us -> 83.4 us
    pallas_call x1, Pallas kernels: 90.6 us -> 83.4 us  [per_device(): pl.pallas_call(functools.partial(kernel, (nt, nr, nc, rl)), out_shape=(ja...]
where the time goes in v5:
time: 90.1 us; the launch traced here: 90 us
  Pallas kernels  83.4 us (93%)
  local copies, waits for them, and re-layouts  5.92 us (7%)
    pallas_call x1, Pallas kernels, per_device(): pl.pallas_call(functools.partial(kernel, (nt, nr, nc, rl)), out_shape=(ja...  83.4 us
    unnamed x19, local copies, waits for them, and re-layouts  5.92 us

profile of v5, /device:TPU:1, one launch (start us, length us, event | category | flops | bytes accessed | tf_op | source)
XLA Modules:
  0.0 90.0 jit_solution(4680620815064618502)
XLA Ops:
  0.6 83.4 %shard_map.126 = (bf16[2048,256]{1,0:T(8,128)(2,1)}, f32[64,256]{1,0:T(8,128)}, f32[1,64]{1,0:T(1,128)}, f32[1,256]{1,0:T(1,128)}, f32[1,256]{1,0:T(1,128)}, /*index=5*/f32[1024,128]{1,0:T(8,128)}, f32[1,128]{1,0:T(1,128)}) custom-call(bf16[2048,256]{1,0:T(8,128)(2,1)} %bitcast.17, f32[1,256]{1,0:T(1,128)} %bitcast.19, f32[1,256]{1,0:T(1,128)} %bitcast.20, ...), custom_call_target="tpu_custom_call" | custom-call | flops 10737418240 | bytes 5242880 | tf_op jit(solution)/shard_map/pallas_call | solution.py:756
  84.0 0.0 copy-start.1
  84.0 0.0 copy-start.5
  84.1 0.0 copy-start.3
  84.1 0.0 copy-start.2
  84.1 0.0 copy-start
  84.1 0.0 copy-start.4
  84.1 2.3 %copy.21 = bf16[1,128,16,256]{3,2,1,0:T(8,128)(2,1)} copy(bf16[1,128,16,256]{3,2,1,0:T(8,128)(2,1)} %bitcast.12) | data formatting | bytes 2097152
  86.4 0.0 copy-done.1
  86.4 0.6 copy.22
  87.0 0.0 copy-done.5
  87.1 0.5 copy.23
  87.6 0.0 copy-done.3
  87.6 0.6 copy.24
  88.1 0.0 copy-done.2
  88.1 0.6 copy.25
  88.7 0.0 copy-done
  88.7 0.8 copy.26
  89.5 0.0 copy-done.4
  89.5 0.5 copy.27
Async XLA Ops:
  84.0 2.4 %copy-start.1 = (f32[64,256]{1,0:T(8,128)S(1)}, f32[64,256]{1,0:T(8,128)}, u32[]{:S(2)}) copy-start(f32[64,256]{1,0:T(8,128)} %get-tuple-element.15) | copy-start | bytes 196612
  84.0 3.0 %copy-start.5 = (f32[1,64]{1,0:T(1,128)S(1)}, f32[1,64]{1,0:T(1,128)}, u32[]{:S(2)}) copy-start(f32[1,64]{1,0:T(1,128)} %get-tuple-element.16) | copy-start | bytes 772
  84.1 3.5 %copy-start.3 = (f32[1,256]{1,0:T(1,128)S(1)}, f32[1,256]{1,0:T(1,128)}, u32[]{:S(2)}) copy-start(f32[1,256]{1,0:T(1,128)} %get-tuple-element.17) | copy-start | bytes 3076
  84.1 4.1 %copy-start.2 = (f32[1,256]{1,0:T(1,128)S(1)}, f32[1,256]{1,0:T(1,128)}, u32[]{:S(2)}) copy-start(f32[1,256]{1,0:T(1,128)} %get-tuple-element.18) | copy-start | bytes 3076
  84.1 4.6 %copy-start = (f32[1024,128]{1,0:T(8,128)S(1)}, f32[1024,128]{1,0:T(8,128)}, u32[]{:S(2)}) copy-start(f32[1024,128]{1,0:T(8,128)} %get-tuple-element.33) | copy-start | bytes 1572868
  84.1 5.4 %copy-start.4 = (f32[1,128]{1,0:T(1,128)S(1)}, f32[1,128]{1,0:T(1,128)}, u32[]{:S(2)}) copy-start(f32[1,128]{1,0:T(1,128)} %get-tuple-element.20) | copy-start | bytes 1540

commit v6 on v5

--- a/solution.py
+++ b/solution.py
@@ -193,14 +193,6 @@
     pt = pm_ref[...]
     bias = jnp.broadcast_to(pb_ref[...], (S, 2 * CH)).T
 
-    wf[...] = w_ref[...].astype(F32)
-
-    def reorder(d, _):
-        rows = wf[pl.ds(d, CH, stride=CH), :]
-        wp[pl.ds(pl.multiple_of(d * CH, CH), CH), :] = rows.astype(BF16)
-        return 0
-
-    lax.fori_loop(0, CH, reorder, 0, unroll=4)
     h_in.wait()
 
     def normalise(k, _):
@@ -320,6 +312,14 @@
     for k in range(2):
         push(*gather_left(k))
 
+    wf[...] = w_ref[...].astype(F32)
+
+    def reorder(d, _):
+        rows = wf[pl.ds(d, CH, stride=CH), :]
+        wp[pl.ds(pl.multiple_of(d * CH, CH), CH), :] = rows.astype(BF16)
+        return 0
+
+    lax.fori_loop(0, CH, reorder, 0, unroll=4)
     g_in.wait()
     obacc[...] = jnp.zeros_like(obacc)
 
@@ -511,9 +511,6 @@
 
     for k in range(2):
         arrived(*near_left(k))
-    for k in range(rpc):
-        unless(z == k, lambda: arrived(*scatter_right_in(k)))
-
     def sum_left(k, _):
         at = pl.ds(pl.multiple_of(k * 128, 128), 128)
         total = lp[c, at, :].astype(F32)
@@ -523,6 +520,9 @@
         return 0
 
     lax.fori_loop(0, lrows // 128, sum_left, 0, unroll=4)
+
+    for k in range(rpc):
+        unless(z == k, lambda: arrived(*scatter_right_in(k)))
 
     def sum_right(k, _):
         at = pl.ds(k * 8, 8)
@@ -583,23 +583,6 @@
         push(*b_row(k))
     b1[r] = sb[r]
 
-    every(arrived, a_part_in)
-    total = a1[0].astype(F32)
-    for q in range(1, group):
-        total += a1[q].astype(F32)
-    a3[t] = total
-
-    def a_tgt(k):
-        q = lax.rem(t + k, nt)
-        return a3.at[t], a3.at[t], a_tgt_send.at[k], a_tgt_recv.at[t], {"tgt": q}
-
-    def a_tgt_in(k):
-        q = lax.rem(t + k, nt)
-        return a3.at[q], a3.at[q], a_tgt_send.at[k], a_tgt_recv.at[q], {"tgt": q}
-
-    for k in range(1, nt):
-        push(*a_tgt(k))
-
     def descend(k, _):
         grad = grads[pl.ds(pl.multiple_of(k * S, S), S), :]
         at = pl.ds(k, S, stride=rl)
@@ -613,6 +596,24 @@
 
     lax.fori_loop(0, rl // 2, descend, 0, unroll=4)
 
+    every(arrived, a_part_in)
+    total = a1[0].astype(F32)
+    for q in range(1, group):
+        total += a1[q].astype(F32)
+    a3[t] = total
+
+    def a_tgt(k):
+        q = lax.rem(t + k, nt)
+        return a3.at[t], a3.at[t], a_tgt_send.at[k], a_tgt_recv.at[t], {"tgt": q}
+
+    def a_tgt_in(k):
+        q = lax.rem(t + k, nt)
+        return a3.at[q], a3.at[q], a_tgt_send.at[k], a_tgt_recv.at[q], {"tgt": q}
+
+    for k in range(1, nt):
+        push(*a_tgt(k))
+
+
     for k in range(1, nr):
         arrived(*b_row_in(k))
     total = b1[0]
@@ -642,6 +643,24 @@
     lax.fori_loop(0, S * rl // 128, emit, 0, unroll=4)
     dx_copy = pltpu.make_async_copy(h, dx_out, local_sem.at[2])
     dx_copy.start()
+
+    for k in range(1, nc):
+        arrived(*b_col_in(k))
+    total = b2[0]
+    for q in range(1, nc):
+        total += b2[q]
+    b3[t] = total
+
+    def b_tgt(k):
+        q = lax.rem(t + k, nt)
+        return b3.at[t], b3.at[t], b_tgt_send.at[k], b_tgt_recv.at[t], {"tgt": q}
+
+    def b_tgt_in(k):
+        q = lax.rem(t + k, nt)
+        return b3.at[q], b3.at[q], b_tgt_send.at[k], b_tgt_recv.at[q], {"tgt": q}
+
+    for k in range(1, nt):
+        push(*b_tgt(k))
 
     for k in range(1, nt):
         arrived(*a_tgt_in(k))
@@ -650,24 +669,6 @@
         total += a3[q]
     a5[flat] = total.astype(BF16)
     every(push, a_whole)
-
-    for k in range(1, nc):
-        arrived(*b_col_in(k))
-    total = b2[0]
-    for q in range(1, nc):
-        total += b2[q]
-    b3[t] = total
-
-    def b_tgt(k):
-        q = lax.rem(t + k, nt)
-        return b3.at[t], b3.at[t], b_tgt_send.at[k], b_tgt_recv.at[t], {"tgt": q}
-
-    def b_tgt_in(k):
-        q = lax.rem(t + k, nt)
-        return b3.at[q], b3.at[q], b_tgt_send.at[k], b_tgt_recv.at[q], {"tgt": q}
-
-    for k in range(1, nt):
-        push(*b_tgt(k))
 
     for k in range(1, nt):
         arrived(*b_tgt_in(k))

time: 90.1 us -> 87.9 us (0.976)
  Pallas kernels: 83.4 us -> 81.2 us
    pallas_call x1, Pallas kernels: 83.4 us -> 81.2 us  [per_device(): pl.pallas_call(functools.partial(kernel, (nt, nr, nc, rl)), out_shape=(ja...]
where the time goes in v6:
time: 87.9 us; the launch traced here: 87.8 us
  Pallas kernels  81.2 us (92%)
  local copies, waits for them, and re-layouts  5.92 us (7%)
    pallas_call x1, Pallas kernels, per_device(): pl.pallas_call(functools.partial(kernel, (nt, nr, nc, rl)), out_shape=(ja...  81.2 us
    unnamed x19, local copies, waits for them, and re-layouts  5.92 us

profile of v6, /device:TPU:1, one launch (start us, length us, event | category | flops | bytes accessed | tf_op | source)
XLA Modules:
  0.0 87.8 jit_solution(9844209578187862495)
XLA Ops:
  0.6 81.2 %shard_map.126 = (bf16[2048,256]{1,0:T(8,128)(2,1)}, f32[64,256]{1,0:T(8,128)}, f32[1,64]{1,0:T(1,128)}, f32[1,256]{1,0:T(1,128)}, f32[1,256]{1,0:T(1,128)}, /*index=5*/f32[1024,128]{1,0:T(8,128)}, f32[1,128]{1,0:T(1,128)}) custom-call(bf16[2048,256]{1,0:T(8,128)(2,1)} %bitcast.17, f32[1,256]{1,0:T(1,128)} %bitcast.19, f32[1,256]{1,0:T(1,128)} %bitcast.20, ...), custom_call_target="tpu_custom_call" | custom-call | flops 10737418240 | bytes 5242880 | tf_op jit(solution)/shard_map/pallas_call | solution.py:757
  81.8 0.0 copy-start.1
  81.8 0.0 copy-start.5
  81.9 0.0 copy-start.3
  81.9 0.0 copy-start.2
  81.9 0.0 copy-start
  81.9 0.0 copy-start.4
  81.9 2.3 %copy.21 = bf16[1,128,16,256]{3,2,1,0:T(8,128)(2,1)} copy(bf16[1,128,16,256]{3,2,1,0:T(8,128)(2,1)} %bitcast.12) | data formatting | bytes 2097152
  84.2 0.0 copy-done.1
  84.2 0.6 copy.22
  84.8 0.0 copy-done.5
  84.8 0.5 copy.23
  85.4 0.0 copy-done.3
  85.4 0.6 copy.24
  85.9 0.0 copy-done.2
  85.9 0.6 copy.25
  86.5 0.0 copy-done
  86.5 0.8 copy.26
  87.3 0.0 copy-done.4
  87.3 0.5 copy.27
Async XLA Ops:
  81.8 2.4 %copy-start.1 = (f32[64,256]{1,0:T(8,128)S(1)}, f32[64,256]{1,0:T(8,128)}, u32[]{:S(2)}) copy-start(f32[64,256]{1,0:T(8,128)} %get-tuple-element.15) | copy-start | bytes 196612
  81.8 3.0 %copy-start.5 = (f32[1,64]{1,0:T(1,128)S(1)}, f32[1,64]{1,0:T(1,128)}, u32[]{:S(2)}) copy-start(f32[1,64]{1,0:T(1,128)} %get-tuple-element.16) | copy-start | bytes 772
  81.9 3.5 %copy-start.3 = (f32[1,256]{1,0:T(1,128)S(1)}, f32[1,256]{1,0:T(1,128)}, u32[]{:S(2)}) copy-start(f32[1,256]{1,0:T(1,128)} %get-tuple-element.17) | copy-start | bytes 3076
  81.9 4.1 %copy-start.2 = (f32[1,256]{1,0:T(1,128)S(1)}, f32[1,256]{1,0:T(1,128)}, u32[]{:S(2)}) copy-start(f32[1,256]{1,0:T(1,128)} %get-tuple-element.18) | copy-start | bytes 3076
  81.9 4.6 %copy-start = (f32[1024,128]{1,0:T(8,128)S(1)}, f32[1024,128]{1,0:T(8,128)}, u32[]{:S(2)}) copy-start(f32[1024,128]{1,0:T(8,128)} %get-tuple-element.33) | copy-start | bytes 1572868
  81.9 5.4 %copy-start.4 = (f32[1,128]{1,0:T(1,128)S(1)}, f32[1,128]{1,0:T(1,128)}, u32[]{:S(2)}) copy-start(f32[1,128]{1,0:T(1,128)} %get-tuple-element.20) | copy-start | bytes 1540

commit v7 on v6

--- a/solution.py
+++ b/solution.py
@@ -206,7 +206,7 @@
         inv[rows, :] = jnp.broadcast_to(scale, (128, 128))
         return 0
 
-    lax.fori_loop(0, S * rl // 128, normalise, 0, unroll=4)
+    lax.fori_loop(0, S * rl // 128, normalise, 0, unroll=8)
 
     def project(k, _):
         at = pl.ds(k, S, stride=rl)
@@ -218,13 +218,13 @@
         rf[pl.ds(pl.multiple_of(k * CH, CH), CH), :] = y[CH:].astype(F32)
         return 0
 
-    lax.fori_loop(0, rl, project, 0, unroll=4)
+    lax.fori_loop(0, rl, project, 0, unroll=8)
 
     def turn(d, _):
         rown[d] = rf[pl.ds(d, rl, stride=CH), :].astype(BF16)
         return 0
 
-    lax.fori_loop(0, CH, turn, 0, unroll=4)
+    lax.fori_loop(0, CH, turn, 0, unroll=8)
     meet(nt, nr, nc)
 
     def xs(k):
@@ -358,7 +358,7 @@
         lmat[:, at] = lt[at, :].T
         return 0
 
-    lax.fori_loop(0, ni * CH // 128, flip, 0, unroll=4)
+    lax.fori_loop(0, ni * CH // 128, flip, 0, unroll=8)
 
     def right_step(k, _):
         lanes = pl.ds(pl.multiple_of(k * 8 * nj, 8 * nj), 8 * nj)
@@ -554,7 +554,7 @@
         acc[:, CM : 2 * CM] += jnp.sum(grad.reshape(S // 8, 8, CM), 0)
         return 0
 
-    lax.fori_loop(0, rl, finish, 0, unroll=4)
+    lax.fori_loop(0, rl, finish, 0, unroll=8)
 
     pr = 2 * 2 * CH // nr
     vr = 8 // nr
@@ -594,7 +594,7 @@
         nrm[1, at, :] = dx[:, 128:] * scale
         return 0
 
-    lax.fori_loop(0, rl // 2, descend, 0, unroll=4)
+    lax.fori_loop(0, rl // 2, descend, 0, unroll=8)
 
     every(arrived, a_part_in)
     total = a1[0].astype(F32)
@@ -632,7 +632,7 @@
     for k in range(1, nc):
         push(*b_col(k))
 
-    lax.fori_loop(rl // 2, rl, descend, 0, unroll=4)
+    lax.fori_loop(rl // 2, rl, descend, 0, unroll=8)
 
     def emit(k, _):
         rows = pl.ds(pl.multiple_of(k * 128, 128), 128)

time: 87.9 us -> 87.4 us (level)
  no operation moved by 1% of the time
where the time goes in v7:
time: 87.4 us; the launch traced here: 87.3 us
  Pallas kernels  80.7 us (92%)
  local copies, waits for them, and re-layouts  5.92 us (7%)
    pallas_call x1, Pallas kernels, per_device(): pl.pallas_call(functools.partial(kernel, (nt, nr, nc, rl)), out_shape=(ja...  80.7 us
    unnamed x19, local copies, waits for them, and re-layouts  5.92 us

profile of v7, /device:TPU:1, one launch (start us, length us, event | category | flops | bytes accessed | tf_op | source)
XLA Modules:
  0.0 87.3 jit_solution(6596356985262948770)
XLA Ops:
  0.6 80.7 %shard_map.126 = (bf16[2048,256]{1,0:T(8,128)(2,1)}, f32[64,256]{1,0:T(8,128)}, f32[1,64]{1,0:T(1,128)}, f32[1,256]{1,0:T(1,128)}, f32[1,256]{1,0:T(1,128)}, /*index=5*/f32[1024,128]{1,0:T(8,128)}, f32[1,128]{1,0:T(1,128)}) custom-call(bf16[2048,256]{1,0:T(8,128)(2,1)} %bitcast.17, f32[1,256]{1,0:T(1,128)} %bitcast.19, f32[1,256]{1,0:T(1,128)} %bitcast.20, ...), custom_call_target="tpu_custom_call" | custom-call | flops 10737418240 | bytes 5242880 | tf_op jit(solution)/shard_map/pallas_call | solution.py:757
  81.3 0.0 copy-start.1
  81.3 0.0 copy-start.5
  81.3 0.0 copy-start.3
  81.3 0.0 copy-start.2
  81.4 0.0 copy-start
  81.4 0.0 copy-start.4
  81.4 2.3 %copy.21 = bf16[1,128,16,256]{3,2,1,0:T(8,128)(2,1)} copy(bf16[1,128,16,256]{3,2,1,0:T(8,128)(2,1)} %bitcast.12) | data formatting | bytes 2097152
  83.7 0.0 copy-done.1
  83.7 0.6 copy.22
  84.3 0.0 copy-done.5
  84.3 0.5 copy.23
  84.8 0.0 copy-done.3
  84.8 0.6 copy.24
  85.4 0.0 copy-done.2
  85.4 0.6 copy.25
  86.0 0.0 copy-done
  86.0 0.8 copy.26
  86.8 0.0 copy-done.4
  86.8 0.5 copy.27
Async XLA Ops:
  81.3 2.4 %copy-start.1 = (f32[64,256]{1,0:T(8,128)S(1)}, f32[64,256]{1,0:T(8,128)}, u32[]{:S(2)}) copy-start(f32[64,256]{1,0:T(8,128)} %get-tuple-element.15) | copy-start | bytes 196612
  81.3 3.0 %copy-start.5 = (f32[1,64]{1,0:T(1,128)S(1)}, f32[1,64]{1,0:T(1,128)}, u32[]{:S(2)}) copy-start(f32[1,64]{1,0:T(1,128)} %get-tuple-element.16) | copy-start | bytes 772
  81.3 3.5 %copy-start.3 = (f32[1,256]{1,0:T(1,128)S(1)}, f32[1,256]{1,0:T(1,128)}, u32[]{:S(2)}) copy-start(f32[1,256]{1,0:T(1,128)} %get-tuple-element.17) | copy-start | bytes 3076
  81.3 4.1 %copy-start.2 = (f32[1,256]{1,0:T(1,128)S(1)}, f32[1,256]{1,0:T(1,128)}, u32[]{:S(2)}) copy-start(f32[1,256]{1,0:T(1,128)} %get-tuple-element.18) | copy-start | bytes 3076
  81.4 4.6 %copy-start = (f32[1024,128]{1,0:T(8,128)S(1)}, f32[1024,128]{1,0:T(8,128)}, u32[]{:S(2)}) copy-start(f32[1024,128]{1,0:T(8,128)} %get-tuple-element.33) | copy-start | bytes 1572868
  81.4 5.4 %copy-start.4 = (f32[1,128]{1,0:T(1,128)S(1)}, f32[1,128]{1,0:T(1,128)}, u32[]{:S(2)}) copy-start(f32[1,128]{1,0:T(1,128)} %get-tuple-element.20) | copy-start | bytes 1540
